TPU v7x, 32 devices: a whole 2x2x4 slice. The times are simulated.
32 devices in a mesh: tokens: 8 (over y, x, core), heads: 4 (over z).
Axes of the slice: x: 2, y: 2, z: 4, core: 2. Of those that a mesh axis runs over, the one named last changes fastest.
Arguments:
- inputs: bfloat16 [4096, 2048], P('tokens'), may hold values from -6 to 6
- segments: int32 [4096], P('tokens'), may hold values from 0 to 7, as said below
- pre_gain: bfloat16 [2048], P('tokens'), may hold values from 0.099609375 to 1.8984375
- mid_gain: bfloat16 [2048], P('tokens'), may hold values from 0.099609375 to 1.8984375
- query_weight: bfloat16 [2048, 2048], P('tokens', 'heads'), may hold values from -0.125 to 0.125
- key_weight: bfloat16 [2048, 256], P('tokens', 'heads'), may hold values from -0.125 to 0.125
- value_weight: bfloat16 [2048, 256], P('tokens', 'heads'), may hold values from -0.125 to 0.125
- out_weight: bfloat16 [2048, 2048], P('heads', 'tokens'), may hold values from -0.5 to 0.5
- gate_weight: bfloat16 [2048, 5632], P('tokens', 'heads'), may hold values from -0.125 to 0.125
- up_weight: bfloat16 [2048, 5632], P('tokens', 'heads'), may hold values from -0.125 to 0.125
- down_weight: bfloat16 [5632, 2048], P('heads', 'tokens'), may hold values from -0.109375 to 0.109375
- cotangent: bfloat16 [4096, 2048], P('tokens'), may hold values from -6 to 6
Outputs:
- layer_out: bfloat16 [4096, 2048], P('tokens')
- grad_input: bfloat16 [4096, 2048], P('tokens')
- grad_pre: float32 [2048], P('tokens')
- grad_mid: float32 [2048], P('tokens')
- grad_query: float32 [2048, 2048], P('tokens', 'heads')
- grad_key: float32 [2048, 256], P('tokens', 'heads')
- grad_value: float32 [2048, 256], P('tokens', 'heads')
- grad_out: float32 [2048, 2048], P('heads', 'tokens')
- grad_gate: float32 [2048, 5632], P('tokens', 'heads')
- grad_up: float32 [2048, 5632], P('tokens', 'heads')
- grad_down: float32 [5632, 2048], P('heads', 'tokens')
Inputs may be any that keep to these rules, and one draw needn't show every extreme that they name: `segments`: segment ids never fall and rise by at most 1 from one token to the next; row r holds exactly the four documents 4 r to 4 r + 3, of uneven lengths; in one row drawn from the seed a document begins within the row's first 512 tokens and ends within its last 512.
All inputs are finite; a program needn't handle non-finite values.
Results may differ from a plain program's by a relative error of at most 0.025.
Values may be sent and summed in bfloat16 or wider, within the bound.
A program may use at most 192 MiB of HBM per device.

v0:
```python
import math

import jax
import jax.numpy as jnp
from jax import lax
from jax.sharding import PartitionSpec as P

ROW = 2048


def rms_scale(vectors):
    return lax.rsqrt(jnp.mean(vectors * vectors, axis=-1, keepdims=True) + 1e-05)


def rotate(vectors, cos_table, sin_table):
    middle_index = vectors.shape[-1] // 2
    former = vectors[..., :middle_index]
    latter = vectors[..., middle_index:]
    return jnp.concatenate(
        [former * cos_table - latter * sin_table, latter * cos_table + former * sin_table], axis=-1
    )


def unrotate(gradient, cos_table, sin_table):
    middle_index = gradient.shape[-1] // 2
    former = gradient[..., :middle_index]
    latter = gradient[..., middle_index:]
    return jnp.concatenate(
        [former * cos_table + latter * sin_table, latter * cos_table - former * sin_table], axis=-1
    )


def norm_back(gradient, vectors, scale_rows, gain_row):
    shaped = vectors * scale_rows
    weighted = gradient * gain_row
    back_vectors = scale_rows * (
        weighted - shaped * jnp.mean(weighted * shaped, axis=-1, keepdims=True)
    )
    return (back_vectors, jnp.sum(gradient * shaped, axis=0))


def shards(
    inputs,
    segments,
    pre_gain,
    mid_gain,
    query_weight,
    key_weight,
    value_weight,
    out_weight,
    gate_weight,
    up_weight,
    down_weight,
    cotangent,
):
    row_count = inputs.shape[0]
    head_size = key_weight.shape[1]
    heads_here = query_weight.shape[1] // head_size
    myself = lax.axis_index("tokens")
    gathered = (
        lax.all_gather(pre_gain, "tokens", axis=0, tiled=True),
        lax.all_gather(mid_gain, "tokens", axis=0, tiled=True),
        lax.all_gather(query_weight, "tokens", axis=0, tiled=True),
        lax.all_gather(key_weight, "tokens", axis=0, tiled=True),
        lax.all_gather(value_weight, "tokens", axis=0, tiled=True),
        lax.all_gather(out_weight, "tokens", axis=1, tiled=True),
        lax.all_gather(gate_weight, "tokens", axis=0, tiled=True),
        lax.all_gather(up_weight, "tokens", axis=0, tiled=True),
        lax.all_gather(down_weight, "tokens", axis=1, tiled=True),
    )
    (
        pre_full,
        mid_full,
        query_full,
        key_full,
        value_full,
        out_full,
        gate_full,
        up_full,
        down_full,
    ) = gathered
    pre_row = pre_full.astype(jnp.float32)
    mid_row = mid_full.astype(jnp.float32)
    all_ids = lax.all_gather(segments, "tokens", axis=0, tiled=True)
    length = all_ids.shape[0]
    places = jnp.arange(length, dtype=jnp.int32)
    starts_here = jnp.concatenate([jnp.ones((1,), dtype=jnp.bool_), all_ids[1:] != all_ids[:-1]])
    opening = lax.cummax(jnp.where(starts_here, places, 0), axis=0)
    own_first = myself * row_count
    positions = lax.dynamic_slice_in_dim(places - opening, own_first, row_count)
    own_places = own_first + jnp.arange(row_count, dtype=jnp.int32)
    half_size = head_size // 2
    inverse = 10000.0 ** (-jnp.arange(half_size, dtype=jnp.float32) / half_size)
    turned = positions.astype(jnp.float32)[:, None] * inverse[None, :]
    cos_table = jnp.cos(turned)[:, None, :]
    sin_table = jnp.sin(turned)[:, None, :]
    inputs_f = inputs.astype(jnp.float32)
    pre_scale = rms_scale(inputs_f)
    normed = (inputs_f * pre_scale * pre_row).astype(jnp.bfloat16)
    queries = jnp.dot(normed, query_full, preferred_element_type=jnp.float32).reshape(
        row_count, heads_here, head_size
    )
    query_rot = (rotate(queries, cos_table, sin_table) * head_size ** (-0.5)).astype(jnp.bfloat16)
    key_rows = jnp.dot(normed, key_full, preferred_element_type=jnp.float32)[:, None, :]
    key_rot = rotate(key_rows, cos_table, sin_table)[:, 0, :].astype(jnp.bfloat16)
    value_low = jnp.dot(normed, value_full, preferred_element_type=jnp.float32).astype(jnp.bfloat16)
    key_all, value_all = (
        lax.all_gather(key_rot, "tokens", axis=0, tiled=True),
        lax.all_gather(value_low, "tokens", axis=0, tiled=True),
    )
    span = math.gcd(ROW, 1024)
    row_start = own_first // ROW * ROW
    block_first = row_start // span
    block_total = (own_first + row_count + span - 1) // span

    def key_block(block_index):
        opening_row = block_index * span
        block_keys = lax.dynamic_slice_in_dim(key_all, opening_row, span)
        block_values = lax.dynamic_slice_in_dim(value_all, opening_row, span)
        block_ids = lax.dynamic_slice_in_dim(all_ids, opening_row, span)
        block_places = opening_row + jnp.arange(span, dtype=jnp.int32)
        allowed = (segments[:, None] == block_ids[None, :]) & (
            own_places[:, None] >= block_places[None, :]
        )
        scores = jnp.einsum(
            "qhd,kd->qhk", query_rot, block_keys, preferred_element_type=jnp.float32
        )
        return (opening_row, block_keys, block_values, allowed[:, None, :], scores)

    def forward_step(block_index, state_now):
        row_peak, row_total, running = state_now
        opening_row, block_keys, block_values, allowed, scores = key_block(block_index)
        new_peak = jnp.maximum(row_peak, jnp.max(jnp.where(allowed, scores, -1e30), axis=-1))
        factor = jnp.exp(row_peak - new_peak)
        weights = jnp.where(allowed, jnp.exp(scores - new_peak[..., None]), 0.0)
        row_total = row_total * factor + jnp.sum(weights, axis=-1)
        running = running * factor[..., None] + jnp.einsum(
            "qhk,kd->qhd",
            weights.astype(jnp.bfloat16),
            block_values,
            preferred_element_type=jnp.float32,
        )
        return (new_peak, row_total, running)

    start_state = (
        jnp.full((row_count, heads_here), -1e30, jnp.float32),
        jnp.zeros((row_count, heads_here), jnp.float32),
        jnp.zeros((row_count, heads_here, head_size), jnp.float32),
    )
    row_peak, row_total, running = lax.fori_loop(
        block_first, block_total, forward_step, start_state
    )
    attended = running / row_total[..., None]
    log_total = row_peak + jnp.log(row_total)
    attended_low = attended.astype(jnp.bfloat16).reshape(row_count, heads_here * head_size)
    attn_term = jnp.dot(attended_low, out_full, preferred_element_type=jnp.float32)
    middle = inputs_f + lax.psum(attn_term.astype(jnp.bfloat16), "heads").astype(jnp.float32)
    mid_scale = rms_scale(middle)
    normed_mid = (middle * mid_scale * mid_row).astype(jnp.bfloat16)
    gate_rows = jnp.dot(normed_mid, gate_full, preferred_element_type=jnp.float32)
    up_rows = jnp.dot(normed_mid, up_full, preferred_element_type=jnp.float32)
    sigmoid_rows = jax.nn.sigmoid(gate_rows)
    silu_rows = gate_rows * sigmoid_rows
    hidden = (silu_rows * up_rows).astype(jnp.bfloat16)
    mlp_term = jnp.dot(hidden, down_full, preferred_element_type=jnp.float32)
    layer_out = (
        middle + lax.psum(mlp_term.astype(jnp.bfloat16), "heads").astype(jnp.float32)
    ).astype(jnp.bfloat16)
    grad_down = jnp.einsum("tf,td->fd", hidden, cotangent, preferred_element_type=jnp.float32)
    back_hidden = jnp.einsum("td,fd->tf", cotangent, down_full, preferred_element_type=jnp.float32)
    back_gate = (
        back_hidden * up_rows * sigmoid_rows * (1.0 + gate_rows * (1.0 - sigmoid_rows))
    ).astype(jnp.bfloat16)
    back_up = (back_hidden * silu_rows).astype(jnp.bfloat16)
    grad_gate = jnp.einsum("tc,tf->cf", normed_mid, back_gate, preferred_element_type=jnp.float32)
    grad_up = jnp.einsum("tc,tf->cf", normed_mid, back_up, preferred_element_type=jnp.float32)
    mid_term = jnp.einsum(
        "tf,cf->tc", back_gate, gate_full, preferred_element_type=jnp.float32
    ) + jnp.einsum("tf,cf->tc", back_up, up_full, preferred_element_type=jnp.float32)
    back_normed_mid = lax.psum(mid_term.astype(jnp.bfloat16), "heads").astype(jnp.float32)
    back_middle, grad_mid = norm_back(back_normed_mid, middle, mid_scale, mid_row)
    back_middle = back_middle + cotangent.astype(jnp.float32)
    back_attn = back_middle.astype(jnp.bfloat16)
    grad_out = jnp.einsum("tc,td->cd", attended_low, back_attn, preferred_element_type=jnp.float32)
    back_attended = (
        jnp.einsum("td,cd->tc", back_attn, out_full, preferred_element_type=jnp.float32)
        .astype(jnp.bfloat16)
        .reshape(row_count, heads_here, head_size)
    )
    row_delta = jnp.sum(back_attended.astype(jnp.float32) * attended, axis=-1)

    def backward_step(block_index, state_now):
        back_rows, back_pairs = state_now
        opening_row, block_keys, block_values, allowed, scores = key_block(block_index)
        chances = jnp.where(allowed, jnp.exp(scores - log_total[..., None]), 0.0)
        back_values = jnp.einsum(
            "qhk,qhd->kd",
            chances.astype(jnp.bfloat16),
            back_attended,
            preferred_element_type=jnp.float32,
        )
        back_chances = jnp.einsum(
            "qhd,kd->qhk", back_attended, block_values, preferred_element_type=jnp.float32
        )
        back_scores = (chances * (back_chances - row_delta[..., None])).astype(jnp.bfloat16)
        back_rows = back_rows + jnp.einsum(
            "qhk,kd->qhd", back_scores, block_keys, preferred_element_type=jnp.float32
        )
        back_keys = jnp.einsum(
            "qhk,qhd->kd", back_scores, query_rot, preferred_element_type=jnp.float32
        )
        old_piece = lax.dynamic_slice_in_dim(back_pairs, opening_row, span)
        fresh_piece = old_piece + jnp.concatenate([back_keys, back_values], axis=-1)
        back_pairs = lax.dynamic_update_slice_in_dim(back_pairs, fresh_piece, opening_row, 0)
        return (back_rows, back_pairs)

    start_back = (
        jnp.zeros((row_count, heads_here, head_size), jnp.float32),
        jnp.zeros((length, 2 * head_size), jnp.float32),
    )
    back_rows, back_pairs = lax.fori_loop(block_first, block_total, backward_step, start_back)
    own_pairs = lax.psum_scatter(
        back_pairs.astype(jnp.bfloat16), "tokens", scatter_dimension=0, tiled=True
    ).astype(jnp.float32)
    back_query = (
        (unrotate(back_rows, cos_table, sin_table) * head_size ** (-0.5))
        .astype(jnp.bfloat16)
        .reshape(row_count, heads_here * head_size)
    )
    back_key = unrotate(own_pairs[:, None, :head_size], cos_table, sin_table)[:, 0, :].astype(
        jnp.bfloat16
    )
    back_value = own_pairs[:, head_size:].astype(jnp.bfloat16)
    grad_query = jnp.einsum("tc,tq->cq", normed, back_query, preferred_element_type=jnp.float32)
    grad_key = jnp.einsum("tc,tq->cq", normed, back_key, preferred_element_type=jnp.float32)
    grad_value = jnp.einsum("tc,tq->cq", normed, back_value, preferred_element_type=jnp.float32)
    pre_term = jnp.einsum("tq,cq->tc", back_query, query_full, preferred_element_type=jnp.float32)
    pre_term = pre_term + jnp.einsum(
        "tq,cq->tc", back_key, key_full, preferred_element_type=jnp.float32
    )
    pre_term = pre_term + jnp.einsum(
        "tq,cq->tc", back_value, value_full, preferred_element_type=jnp.float32
    )
    back_normed = lax.psum(pre_term.astype(jnp.bfloat16), "heads").astype(jnp.float32)
    back_inputs, grad_pre = norm_back(back_normed, inputs_f, pre_scale, pre_row)
    grad_input = (back_middle + back_inputs).astype(jnp.bfloat16)
    summed = (
        lax.psum_scatter(
            grad_pre.astype(jnp.bfloat16), "tokens", scatter_dimension=0, tiled=True
        ).astype(jnp.float32),
        lax.psum_scatter(
            grad_mid.astype(jnp.bfloat16), "tokens", scatter_dimension=0, tiled=True
        ).astype(jnp.float32),
        lax.psum_scatter(
            grad_query.astype(jnp.bfloat16), "tokens", scatter_dimension=0, tiled=True
        ).astype(jnp.float32),
        lax.psum_scatter(
            grad_key.astype(jnp.bfloat16), "tokens", scatter_dimension=0, tiled=True
        ).astype(jnp.float32),
        lax.psum_scatter(
            grad_value.astype(jnp.bfloat16), "tokens", scatter_dimension=0, tiled=True
        ).astype(jnp.float32),
        lax.psum_scatter(
            grad_out.astype(jnp.bfloat16), "tokens", scatter_dimension=1, tiled=True
        ).astype(jnp.float32),
        lax.psum_scatter(
            grad_gate.astype(jnp.bfloat16), "tokens", scatter_dimension=0, tiled=True
        ).astype(jnp.float32),
        lax.psum_scatter(
            grad_up.astype(jnp.bfloat16), "tokens", scatter_dimension=0, tiled=True
        ).astype(jnp.float32),
        lax.psum_scatter(
            grad_down.astype(jnp.bfloat16), "tokens", scatter_dimension=1, tiled=True
        ).astype(jnp.float32),
    )
    (
        grad_pre,
        grad_mid,
        grad_query,
        grad_key,
        grad_value,
        grad_out,
        grad_gate,
        grad_up,
        grad_down,
    ) = summed
    return (
        layer_out,
        grad_input,
        grad_pre,
        grad_mid,
        grad_query,
        grad_key,
        grad_value,
        grad_out,
        grad_gate,
        grad_up,
        grad_down,
    )


def solution(mesh):
    return jax.shard_map(
        shards,
        mesh=mesh,
        in_specs=(
            P("tokens", None),
            P("tokens"),
            P("tokens"),
            P("tokens"),
            P("tokens", "heads"),
            P("tokens", "heads"),
            P("tokens", "heads"),
            P("heads", "tokens"),
            P("tokens", "heads"),
            P("tokens", "heads"),
            P("heads", "tokens"),
            P("tokens", None),
        ),
        out_specs=(
            P("tokens", None),
            P("tokens", None),
            P("tokens"),
            P("tokens"),
            P("tokens", "heads"),
            P("tokens", "heads"),
            P("tokens", "heads"),
            P("heads", "tokens"),
            P("tokens", "heads"),
            P("tokens", "heads"),
            P("heads", "tokens"),
        ),
        check_vma=False,
    )
```

profile of v0, /device:TPU:0, one launch (start us, length us, event | category | flops | bytes accessed | tf_op | source)
XLA Modules:
  0.0 1094.5 jit_solution(7872658492659618564)
XLA Ops:
  11.5 10.3 all-gather.2
  21.9 8.9 all-gather.1
  31.6 9.9 all_gather.38
  41.5 9.5 all_gather.41
  54.4 10.2 all_gather.42
  64.7 11.4 %all-gather = bf16[4096,1,64]{0,2,1:T(8,128)(2,1)} all-gather(bf16[512,1,64]{0,2,1:T(8,128)(2,1)S(1)} %pad_maximum_fusion), channel_id=2, replica_groups=mesh['tokens'=8,'heads'=4] {'tokens'}, dimensions={0}, use_global_device_ids=true | all-gather | bytes 589824 | tf_op jit(solution)/shard_map/all_gather | solution.py:108
  76.1 3.5 fusion.93
  81.1 29.0 %while.28 = (s32[]{:T(128)}, f32[512,8]{0,1:T(8,128)S(1)}, f32[512,8]{0,1:T(8,128)S(1)}, f32[512,8,64]{0,2,1:T(8,128)}, s32[]{:T(128)}, /*index=5*/s32[512]{0:T(...) while((s32[]{:T(128)}, f32[512,8]{0,1:T(8,128)S(1)}, ...), condition=%wide.region_6.7_spmd.clone, body=%wide.region_3.6_spmd.clone.sunk | while | flops 1109403136 | bytes 55601356 | solution.py:150
  82.2 9.2 fusion.164
  91.5 8.6 fusion.165
  100.1 9.9 fusion.166
  111.4 4.4 convolution_convert_fusion.5
  117.7 37.3 %all-gather.3 = bf16[8,1,256]{2,1,0:T(2,128)(2,1)S(1)} all-gather(bf16[1,1,256]{2,1,0:T(2,128)(2,1)S(1)} %reshape.293), channel_id=1, replica_groups=mesh['tokens'=8,'heads'=4] {'tokens'}, dimensions={0}, use_global_device_ids=true | all-gather | bytes 4608 | tf_op jit(solution)/shard_map/all_gather | solution.py:62
  154.9 76.5 %all-reduce.8.cloned.1.call-done = bf16[512,2048]{1,0:T(8,128)(2,1)} async-done(((bf16[512,2048]{1,0:T(8,128)(2,1)}), bf16[512,2048]{1,0:T(8,128)(2,1)}) %all-reduce.8.cloned.1.call-update) | async-done | bytes 2097168 | tf_op jit(solution)/shard_map/psum | solution.py:157
  236.3 39.3 %all-gather.16.cloned.1.call-done = bf16[2048,1408]{1,0:T(8,128)(2,1)} async-done(((bf16[256,1408]{1,0:T(8,128)(2,1)}), bf16[2048,1408]{1,0:T(8,128)(2,1)}) %all-gather.16.cloned.1.call-update) | async-done | bytes 5767184 | tf_op jit(solution)/shard_map/all_gather | solution.py:68
  275.6 8.3 fusion.95
  283.9 36.9 %all-gather.14.cloned.1.call-done = bf16[2048,1408]{1,0:T(8,128)(2,1)} async-done(((bf16[256,1408]{1,0:T(8,128)(2,1)}), bf16[2048,1408]{1,0:T(8,128)(2,1)}) %all-gather.14.cloned.1.call-update) | async-done | bytes 5767184 | tf_op jit(solution)/shard_map/all_gather | solution.py:67
  320.9 8.3 fusion.94
  329.1 38.0 %all-gather.18.cloned.1.call-done = bf16[1408,2048]{1,0:T(8,128)(2,1)} async-done(((bf16[1408,256]{1,0:T(8,128)(2,1)}), bf16[1408,2048]{1,0:T(8,128)(2,1)}) %all-gather.18.cloned.1.call-update) | async-done | bytes 5767184 | tf_op jit(solution)/shard_map/all_gather | solution.py:69
  367.1 10.5 multiply_convert_fusion.1
  377.7 3.4 fusion.96
  381.1 7.6 add_convert_fusion.1
  388.8 86.6 %all-reduce.10.cloned.1.call-done = bf16[512,2048]{1,0:T(8,128)(2,1)} async-done(((bf16[512,2048]{1,0:T(8,128)(2,1)}), bf16[512,2048]{1,0:T(8,128)(2,1)}) %all-reduce.10.cloned.1.call-update) | async-done | bytes 2097168 | tf_op jit(solution)/shard_map/psum | solution.py:180
  475.4 4.5 fusion.56
  480.0 5.1 multiply_reduce_fusion.1
  487.8 25.9 %while.29 = (s32[]{:T(128)}, f32[512,8,64]{0,2,1:T(8,128)}, f32[4096,128]{0,1:T(8,128)}, s32[]{:T(128)}, s32[512]{0:T(512)S(1)}, /*index=5*/s32[4096]{0:T(1024)S...) while((s32[]{:T(128)}, f32[512,8,64]{0,2,1:T(8,128)}, ...), condition=%wide.region_14.15_spmd.clone, body=%wide.region_13.14_spmd.clone.sunk | while | flops 2720007680 | bytes 119482656 | solution.py:221
  491.1 3.0 fusion.179
  494.0 7.6 fusion.178
  501.6 6.1 convolution_bitcast_fusion.3
  507.8 3.8 convolution_add_fusion.2
  513.8 2.9 convert_element_type.187
  516.7 60.8 %reduce-scatter.9.cloned.1.call-done = bf16[512,128]{0,1:T(8,128)(2,1)} async-done(((bf16[4096,128]{0,1:T(8,128)(2,1)}), bf16[512,128]{0,1:T(8,128)(2,1)}) %reduce-scatter.9.cloned.1.call-update) | async-done | bytes 131088 | tf_op jit(solution)/shard_map/reduce_scatter | solution.py:222
  584.7 4.4 convolution_convert_fusion.4
  589.2 6.4 convolution_convert_fusion.3
  595.7 8.0 convolution_convert_fusion.6
  608.5 7.7 convolution_convert_fusion
  616.3 8.0 convolution_convert_fusion.1
  624.4 8.0 convolution_convert_fusion.2
  635.7 15.2 %reduce-scatter.15.cloned.1.call-done = bf16[256,64]{0,1:T(8,128)(2,1)} async-done(((bf16[2048,64]{0,1:T(8,128)(2,1)}), bf16[256,64]{0,1:T(8,128)(2,1)}) %reduce-scatter.15.cloned.1.call-update) | async-done | bytes 32784 | tf_op jit(solution)/shard_map/reduce_scatter | solution.py:260
  652.3 43.2 %reduce-scatter.11.cloned.1.call-done = bf16[256,512]{1,0:T(8,128)(2,1)} async-done(((bf16[2048,512]{1,0:T(8,128)(2,1)}), bf16[256,512]{1,0:T(8,128)(2,1)}) %reduce-scatter.11.cloned.1.call-update) | async-done | bytes 262160 | tf_op jit(solution)/shard_map/reduce_scatter | solution.py:254
  697.3 42.9 %reduce-scatter.17.cloned.1.call-done = bf16[512,256]{1,0:T(8,128)(2,1)} async-done(((bf16[512,2048]{1,0:T(8,128)(2,1)}), bf16[512,256]{1,0:T(8,128)(2,1)}) %reduce-scatter.17.cloned.1.call-update) | async-done | bytes 262160 | tf_op jit(solution)/shard_map/reduce_scatter | solution.py:263
  742.0 156.6 %all-reduce.12.cloned.1.call-done = (bf16[512,2048]{1,0:T(8,128)(2,1)}, bf16[512,2048]{1,0:T(8,128)(2,1)}) async-done(((bf16[512,2048]{1,0:T(8,128)(2,1)}, bf16[512,2048]{1,0:T(8,128)(2,1)}), (bf16[512,2048]{1,0:T(8,128)(2,1)}, bf16[512,2048]{1,0:T(8,128)(2,1)})) %all-reduce.12.cloned.1.call-update) | async-done | bytes 4194320 | tf_op jit(solution)/shard_map/psum | solution.py:167
  898.6 2.9 fusion.59
  901.5 14.1 %all-reduce.2 = (bf16[2048]{0:T(1024)(128)(2,1)S(1)}, bf16[2048]{0:T(1024)(128)(2,1)S(1)}) all-reduce(bf16[2048]{0:T(1024)(128)(2,1)S(1)} %get-tuple-element.203, bf16[2048]{0:T(1024)(128)(2,1)S(1)} %copy-done.36), channel_id=4, replica_groups=mesh['tokens'=8,'heads'=4] {'tokens'}, use_global_device_ids=true, to_apply=%region_19.20.clone | all-reduce | flops 4096 | bytes 16384
  916.3 8.1 fusion.52
  924.3 36.0 %reduce-scatter.23.cloned.1.call-done = bf16[1408,256]{1,0:T(8,128)(2,1)} async-done(((bf16[1408,2048]{1,0:T(8,128)(2,1)}), bf16[1408,256]{1,0:T(8,128)(2,1)}) %reduce-scatter.23.cloned.1.call-update) | async-done | bytes 720912 | tf_op jit(solution)/shard_map/reduce_scatter | solution.py:272
  962.7 60.0 %reduce-scatter.21.cloned.1.call-done = bf16[256,1408]{1,0:T(8,128)(2,1)} async-done(((bf16[2048,1408]{1,0:T(8,128)(2,1)}), bf16[256,1408]{1,0:T(8,128)(2,1)}) %reduce-scatter.21.cloned.1.call-update) | async-done | bytes 720912 | tf_op jit(solution)/shard_map/reduce_scatter | solution.py:269
  1025.0 60.5 %reduce-scatter.19.cloned.1.call-done = bf16[256,1408]{1,0:T(8,128)(2,1)} async-done(((bf16[2048,1408]{1,0:T(8,128)(2,1)}), bf16[256,1408]{1,0:T(8,128)(2,1)}) %reduce-scatter.19.cloned.1.call-update) | async-done | bytes 720912 | tf_op jit(solution)/shard_map/reduce_scatter | solution.py:266
  (189 shorter events, 54.1 us)
Async XLA Ops:
  7.2 43.9 %copy-start.1 = (bf16[512,2048]{1,0:T(8,128)(2,1)S(1)}, bf16[512,2048]{1,0:T(8,128)(2,1)}, u32[]{:S(2)}) copy-start(bf16[512,2048]{1,0:T(8,128)(2,1)} %param.16) | copy-start | bytes 6291460
  7.2 68.9 %all-gather.10.cloned.1.call-start = ((), (), s32[]{:S(2)}) async-start(), calls=%async_computation.8 | async-start | bytes 2359296 | tf_op jit(solution)/shard_map/all_gather | solution.py:63
  7.9 103.5 %all-gather.12.cloned.1.call-start = ((), (), s32[]{:S(2)}) async-start(), calls=%async_computation.9 | async-start | bytes 2359296 | tf_op jit(solution)/shard_map/all_gather | solution.py:66
  8.7 222.7 %all-reduce.8.cloned.1.call-start = ((), (), s32[]{:S(2)}) async-start(), calls=%async_computation.10 | async-start | bytes 4194304 | tf_op jit(solution)/shard_map/psum | solution.py:157
  8.8 45.3 %copy-start.37 = (f32[32]{0:T(128)}, f32[32]{0:T(128)S(1)}, u32[]{:S(2)}) copy-start(f32[32]{0:T(128)S(1)} %multiply_power_fusion) | copy-start | bytes 388
  11.5 42.1 %copy-start.30 = (f32[512]{0:T(512)}, f32[512]{0:T(512)S(1)}, u32[]{:S(2)}) copy-start(f32[512]{0:T(512)S(1)} %add_rsqrt_fusion.1) | copy-start | bytes 6148
  21.9 31.8 %copy-start.26 = (f32[8,1,256]{2,1,0:T(1,128)}, f32[8,1,256]{2,1,0:T(1,128)S(1)}, u32[]{:S(2)}) copy-start(f32[8,1,256]{2,1,0:T(1,128)S(1)} %convert_element_type.210) | copy-start | bytes 24580
  41.5 12.2 %copy-start.10 = (bf16[2048,64]{0,1:T(8,128)(2,1)}, bf16[2048,64]{0,1:T(8,128)(2,1)S(1)}, u32[]{:S(2)}) copy-start(bf16[2048,64]{0,1:T(8,128)(2,1)S(1)} %all_gather.38) | copy-start | bytes 786436
  53.8 25.8 %copy-start.32 = (f32[512]{0:T(512)}, f32[512]{0:T(512)S(1)}, u32[]{:S(2)}) copy-start(f32[512]{0:T(512)S(1)} %fusion.88) | copy-start | bytes 6148
  54.1 25.5 %copy-start.15 = (f32[512,32]{0,1:T(8,128)}, f32[512,32]{0,1:T(8,128)S(1)}, u32[]{:S(2)}) copy-start(f32[512,32]{0,1:T(8,128)S(1)} %get-tuple-element.274) | copy-start | bytes 196612
  54.1 25.5 %copy-start.17 = (f32[512,32]{0,1:T(8,128)}, f32[512,32]{0,1:T(8,128)S(1)}, u32[]{:S(2)}) copy-start(f32[512,32]{0,1:T(8,128)S(1)} %get-tuple-element.275) | copy-start | bytes 196612
  111.4 5.0 copy-start.19
  111.4 6.2 copy-start.40
  115.8 159.8 %all-gather.16.cloned.1.call-start = ((), (), s32[]{:S(2)}) async-start(), calls=%async_computation.12 | async-start | bytes 6488064 | tf_op jit(solution)/shard_map/all_gather | solution.py:68
  116.4 204.4 %all-gather.14.cloned.1.call-start = ((), (), s32[]{:S(2)}) async-start(), calls=%async_computation.11 | async-start | bytes 6488064 | tf_op jit(solution)/shard_map/all_gather | solution.py:67
  117.0 250.1 %all-gather.18.cloned.1.call-start = ((), (), s32[]{:S(2)}) async-start(), calls=%async_computation.13 | async-start | bytes 6488064 | tf_op jit(solution)/shard_map/all_gather | solution.py:69
  117.6 357.8 %all-reduce.10.cloned.1.call-start = ((), (), s32[]{:S(2)}) async-start(), calls=%async_computation.14 | async-start | bytes 4194304 | tf_op jit(solution)/shard_map/psum | solution.py:180
  154.9 325.0 %copy-start.24 = (f32[8,1,256]{2,1,0:T(1,128)}, f32[8,1,256]{2,1,0:T(1,128)S(1)}, u32[]{:S(2)}) copy-start(f32[8,1,256]{2,1,0:T(1,128)S(1)} %convert_element_type.211) | copy-start | bytes 24580
  233.9 246.0 %copy-start.28 = (f32[512]{0:T(512)}, f32[512]{0:T(512)S(1)}, u32[]{:S(2)}) copy-start(f32[512]{0:T(512)S(1)} %add_rsqrt_fusion) | copy-start | bytes 6148
  367.1 10.5 copy-start.39
  388.7 188.7 %reduce-scatter.9.cloned.1.call-start = ((), (), s32[]{:S(2)}) async-start(), calls=%async_computation.15 | async-start | bytes 1179648 | tf_op jit(solution)/shard_map/reduce_scatter | solution.py:222
  475.4 4.5 copy-start.8
  480.0 5.2 copy-start.34
  480.0 7.8 copy-start.9
  501.6 6.2 copy-start
  513.7 64.7 %copy-start.33 = (f32[512]{0:T(512)S(1)}, f32[512]{0:T(512)}, u32[]{:S(2)}) copy-start(f32[512]{0:T(512)} %copy-done.32) | copy-start | bytes 6148
  513.7 64.7 %copy-start.38 = (f32[32]{0:T(128)S(1)}, f32[32]{0:T(128)}, u32[]{:S(2)}) copy-start(f32[32]{0:T(128)} %copy-done.37) | copy-start | bytes 388
  513.7 65.0 %copy-start.7 = (bf16[512,2048]{1,0:T(8,128)(2,1)S(1)}, bf16[512,2048]{1,0:T(8,128)(2,1)}, u32[]{:S(2)}) copy-start(bf16[512,2048]{1,0:T(8,128)(2,1)} %copy-done.6) | copy-start | bytes 6291460
  513.7 66.3 %copy-start.16 = (f32[512,32]{0,1:T(8,128)S(1)}, f32[512,32]{0,1:T(8,128)}, u32[]{:S(2)}) copy-start(f32[512,32]{0,1:T(8,128)} %copy-done.15) | copy-start | bytes 196612
  513.8 66.3 %copy-start.18 = (f32[512,32]{0,1:T(8,128)S(1)}, f32[512,32]{0,1:T(8,128)}, u32[]{:S(2)}) copy-start(f32[512,32]{0,1:T(8,128)} %copy-done.17) | copy-start | bytes 196612
  516.7 117.6 %reduce-scatter.13.cloned.1.call-start = ((), (), s32[]{:S(2)}) async-start(), calls=%async_computation.17 | async-start | bytes 294912 | tf_op jit(solution)/shard_map/reduce_scatter | solution.py:257
  577.5 4.7 copy-start.22
  580.0 70.9 %reduce-scatter.15.cloned.1.call-start = ((), (), s32[]{:S(2)}) async-start(), calls=%async_computation.18 | async-start | bytes 294912 | tf_op jit(solution)/shard_map/reduce_scatter | solution.py:260
  583.4 112.0 %reduce-scatter.11.cloned.1.call-start = ((), (), s32[]{:S(2)}) async-start(), calls=%async_computation.16 | async-start | bytes 2359296 | tf_op jit(solution)/shard_map/reduce_scatter | solution.py:254
  584.6 4.5 copy-start.2
  584.7 4.5 copy-start.20
  584.7 4.5 copy-start.25
  584.7 4.5 copy-start.29
  584.7 4.5 copy-start.35
  589.1 151.1 %reduce-scatter.17.cloned.1.call-start = ((), (), s32[]{:S(2)}) async-start(), calls=%async_computation.19 | async-start | bytes 2359296 | tf_op jit(solution)/shard_map/reduce_scatter | solution.py:263
  595.6 303.0 %all-reduce.12.cloned.1.call-start = ((), (), s32[]{:S(2)}) async-start(), calls=%async_computation.23 | async-start | bytes 8388608 | tf_op jit(solution)/shard_map/psum | solution.py:167
  595.7 8.0 copy-start.14
  608.1 352.2 %reduce-scatter.23.cloned.1.call-start = ((), (), s32[]{:S(2)}) async-start(), calls=%async_computation.22 | async-start | bytes 6488064 | tf_op jit(solution)/shard_map/reduce_scatter | solution.py:272
  616.3 406.4 %reduce-scatter.21.cloned.1.call-start = ((), (), s32[]{:S(2)}) async-start(), calls=%async_computation.21 | async-start | bytes 6488064 | tf_op jit(solution)/shard_map/reduce_scatter | solution.py:269
  624.3 461.1 %reduce-scatter.19.cloned.1.call-start = ((), (), s32[]{:S(2)}) async-start(), calls=%async_computation.20 | async-start | bytes 6488064 | tf_op jit(solution)/shard_map/reduce_scatter | solution.py:266
  632.4 266.2 %copy-start.27 = (f32[8,1,256]{2,1,0:T(1,128)S(1)}, f32[8,1,256]{2,1,0:T(1,128)}, u32[]{:S(2)}) copy-start(f32[8,1,256]{2,1,0:T(1,128)} %copy-done.26) | copy-start | bytes 24580
  632.4 266.2 %copy-start.31 = (f32[512]{0:T(512)S(1)}, f32[512]{0:T(512)}, u32[]{:S(2)}) copy-start(f32[512]{0:T(512)} %copy-done.30) | copy-start | bytes 6148
  632.4 269.1 %copy-start.36 = (bf16[2048]{0:T(1024)(128)(2,1)S(1)}, bf16[2048]{0:T(1024)(128)(2,1)}, u32[]{:S(2)}) copy-start(bf16[2048]{0:T(1024)(128)(2,1)} %get-tuple-element.201) | copy-start | bytes 12292
  (12 other events, 29.3 us)
Sparse Core Ops, SparseCore 0:
  9.9 31.2 all-gather.9
  43.1 28.2 all-gather.11
  116.0 115.4 all-reduce.7
  233.3 42.2 all-gather.15
  277.5 43.3 all-gather.13
  322.7 44.3 all-gather.17
  388.9 86.5 all-reduce.9
  516.8 60.6 reduce-scatter.8
  580.5 33.5 reduce-scatter.12
  617.3 33.5 reduce-scatter.14
  654.2 41.2 reduce-scatter.10
  699.0 41.2 reduce-scatter.16
  743.2 155.3 all-reduce.11
  902.3 58.0 reduce-scatter.22
  963.6 59.0 reduce-scatter.20
  1026.4 59.0 reduce-scatter.18
where the time goes:
time: 1100 us; the launch traced here: 1090 us
  waiting for transfers between devices  756 us (69%)
  matrix products  144 us (13%)
  blocking collectives  112 us (10%)
  other arithmetic  59.6 us (5%)
  between operations  15.5 us (1%)
    psum x1, waiting for transfers between devices, shards(): lax.psum(mlp_term.astype(jnp.bfloat16), 'heads').astype(jnp.float32)  157 us
    psum x1, waiting for transfers between devices, shards(): lax.psum(mid_term.astype(jnp.bfloat16), 'heads').astype(jnp.float32)  86.6 us
    psum x1, waiting for transfers between devices, shards(): lax.psum(attn_term.astype(jnp.bfloat16), 'heads').astype(jnp.float32)  76.5 us
    reduce_scatter x1, waiting for transfers between devices, shards(): lax.psum_scatter(back_pairs.astype(jnp.bfloat16), 'tokens', scatter_dimen...  60.8 us
    reduce_scatter x1, waiting for transfers between devices, shards(): lax.psum_scatter(grad_gate.astype(jnp.bfloat16), 'tokens', scatter_dimens...  60.5 us
    reduce_scatter x1, waiting for transfers between devices, shards(): lax.psum_scatter(grad_up.astype(jnp.bfloat16), 'tokens', scatter_dimensio...  60 us
    reduce_scatter x1, waiting for transfers between devices, shards(): lax.psum_scatter(grad_query.astype(jnp.bfloat16), 'tokens', scatter_dimen...  43.2 us
    reduce_scatter x1, waiting for transfers between devices, shards(): lax.psum_scatter(grad_out.astype(jnp.bfloat16), 'tokens', scatter_dimensi...  42.9 us
  transfers between devices with their start and end apart: 16, of which 13 were waited for; matrix products, arithmetic and copies ran while one was open for 13% of the time, Pallas kernels for 0%

commit v1 on v0

--- a/solution.py
+++ b/solution.py
@@ -1,8 +1,11 @@
+import functools
 import math
 
 import jax
 import jax.numpy as jnp
 from jax import lax
+from jax.experimental import pallas as pl
+from jax.experimental.pallas import tpu as pltpu
 from jax.sharding import PartitionSpec as P
 
 ROW = 2048
@@ -39,7 +42,7 @@
     return (back_vectors, jnp.sum(gradient * shaped, axis=0))
 
 
-def shards(
+def shards_any(
     inputs,
     segments,
     pre_gain,
@@ -299,9 +302,654 @@
     )
 
 
+MESH_ID = pl.DeviceIdType.MESH
+VMEM_BYTES = 60 * 2**20
+
+
+def token_device(flip):
+    return (jnp.bitwise_xor(lax.axis_index("tokens"), flip), lax.axis_index("heads"))
+
+
+def remote(src, dst, send, recv, device):
+    return pltpu.make_async_remote_copy(
+        src_ref=src, dst_ref=dst, send_sem=send, recv_sem=recv, device_id=device, device_id_type=MESH_ID
+    )
+
+
+def greet_cube():
+    barrier = pltpu.get_barrier_semaphore()
+    for flip in (1, 2, 4):
+        pl.semaphore_signal(barrier, inc=1, device_id=token_device(flip), device_id_type=MESH_ID)
+    pl.semaphore_wait(barrier, 3)
+
+
+def block_of(ref, axis, index, half=None):
+    size = ref.shape[axis] // 8
+    start = pl.multiple_of(index * size, size)
+    if axis == 0:
+        if half is None:
+            return ref.at[pl.ds(start, size), :]
+        return ref.at[pl.ds(pl.multiple_of(start + half * (size // 2), size // 2), size // 2), :]
+    if half is None:
+        return ref.at[:, pl.ds(start, size)]
+    rows = ref.shape[0] // 2
+    return ref.at[pl.ds(half * rows, rows), pl.ds(start, size)]
+
+
+class Gather:
+    COPIES = 9
+
+    def __init__(self, shard, full, axis, send, recv):
+        self.shard, self.full, self.axis, self.send, self.recv = shard, full, axis, send, recv
+        self.me = lax.axis_index("tokens")
+
+    def copy(self, slot, flip_block, flip_target, half=None):
+        index = jnp.bitwise_xor(self.me, flip_block)
+        src = self.shard if flip_block == 0 else block_of(self.full, self.axis, index, half)
+        return remote(
+            src,
+            block_of(self.full, self.axis, index, half),
+            self.send.at[slot],
+            self.recv.at[slot],
+            token_device(flip_target),
+        )
+
+    def copies(self, slot):
+        return self.copy(
+            slot,
+            *(
+                (0, 2),
+                (0, 4),
+                (0, 1),
+                (2, 4, 0),
+                (4, 2, 1),
+                (2, 1),
+                (4, 1),
+                (6, 1, 0),
+                (6, 1, 1),
+            )[slot],
+        )
+
+    def start(self, local):
+        for slot in (0, 1, 2):
+            self.copies(slot).start()
+        mine = pltpu.make_async_copy(self.shard, block_of(self.full, self.axis, self.me), local)
+        mine.start()
+        mine.wait()
+
+    def relay(self):
+        self.copies(0).wait_recv()
+        self.copies(3).start()
+        self.copies(1).wait_recv()
+        self.copies(4).start()
+        self.copies(5).start()
+        self.copies(6).start()
+
+    def finish_relay(self):
+        self.copies(3).wait_recv()
+        self.copies(7).start()
+        self.copies(4).wait_recv()
+        self.copies(8).start()
+
+    def finish(self):
+        for slot in (2, 5, 6, 7, 8):
+            self.copies(slot).wait_recv()
+        for slot in range(self.COPIES):
+            self.copies(slot).wait_send()
+
+
+def gather_kernel(axes, *refs):
+    count = len(axes)
+    shards_in, fulls = refs[:count], refs[count : 2 * count]
+    send, recv, local = refs[2 * count :]
+    greet_cube()
+    parts = [
+        Gather(shards_in[i], fulls[i], axes[i], send.at[i], recv.at[i]) for i in range(count)
+    ]
+    ahead = 2
+    for i in range(count + ahead + 1):
+        if i < count:
+            parts[i].start(local.at[i])
+        if 0 <= i - ahead < count:
+            parts[i - ahead].relay()
+        if 0 <= i - ahead - 1 < count:
+            parts[i - ahead - 1].finish_relay()
+    for part in parts:
+        part.finish()
+
+
+def gather_weights(arrays, axes, collective_id):
+    count = len(arrays)
+    shapes = [
+        tuple(size * 8 if d == axis else size for d, size in enumerate(array.shape))
+        for array, axis in zip(arrays, axes)
+    ]
+    return pl.pallas_call(
+        functools.partial(gather_kernel, axes),
+        out_shape=[jax.ShapeDtypeStruct(s, a.dtype) for s, a in zip(shapes, arrays)],
+        in_specs=[pl.BlockSpec(memory_space=pl.ANY)] * count,
+        out_specs=[pl.BlockSpec(memory_space=pl.ANY)] * count,
+        scratch_shapes=[
+            pltpu.SemaphoreType.DMA((count, Gather.COPIES)),
+            pltpu.SemaphoreType.DMA((count, Gather.COPIES)),
+            pltpu.SemaphoreType.DMA((count,)),
+        ],
+        compiler_params=pltpu.CompilerParams(collective_id=collective_id, has_side_effects=True),
+        name="gather_weights",
+    )(*arrays)
+
+
+def greet_chain(chain):
+    here = lax.axis_index("heads")
+    barrier = pltpu.get_barrier_semaphore()
+    for step in (-1, 1):
+        near = here + step
+
+        @pl.when((near >= 0) & (near < chain))
+        def _():
+            pl.semaphore_signal(
+                barrier,
+                inc=1,
+                device_id=(lax.axis_index("tokens"), near),
+                device_id_type=MESH_ID,
+            )
+
+    edge = (here == 0) | (here == chain - 1)
+
+    @pl.when(edge)
+    def _():
+        pl.semaphore_wait(barrier, 1)
+
+    @pl.when(jnp.logical_not(edge))
+    def _():
+        pl.semaphore_wait(barrier, 2)
+
+
+class ChainSum:
+    def __init__(self, chain, upward, term, passing, total, first_row, rows, sems):
+        self.chain, self.term, self.passing, self.total = chain, term, passing, total
+        self.first_row, self.rows = first_row, rows
+        here = lax.axis_index("heads")
+        self.rank = here if upward else chain - 1 - here
+        move = 1 if upward else -1
+        clip = lambda h: jnp.clip(h, 0, chain - 1)
+        tokens = lax.axis_index("tokens")
+        self.ahead = (tokens, clip(here + move))
+        self.behind = (tokens, clip(here - move))
+        self.sems = sems
+        self.first = self.rank == 0
+        self.last = self.rank == chain - 1
+
+    def place(self, i):
+        return pl.ds(self.first_row + i * self.rows, self.rows)
+
+    def out_copy(self, i, first):
+        place = self.place(i)
+        src = self.term if first else self.passing
+        return remote(
+            src.at[place], self.passing.at[place], self.sems.at[0, i], self.sems.at[1, i], self.ahead
+        )
+
+    def back_copy(self, i):
+        place = self.place(i)
+        return remote(
+            self.total.at[place], self.total.at[place], self.sems.at[2, i], self.sems.at[3, i], self.behind
+        )
+
+    def add(self, i):
+        place = self.place(i)
+        return self.term[place, :].astype(jnp.float32) + self.passing[place, :].astype(jnp.float32)
+
+    def out_step(self, i):
+        @pl.when(self.first)
+        def _():
+            self.out_copy(i, True).start()
+
+        @pl.when(jnp.logical_not(self.first))
+        def _():
+            self.out_copy(i, False).wait_recv()
+
+        @pl.when(jnp.logical_not(self.first | self.last))
+        def _():
+            self.passing[self.place(i), :] = self.add(i).astype(self.passing.dtype)
+            self.out_copy(i, False).start()
+
+        @pl.when(self.last)
+        def _():
+            self.total[self.place(i), :] = self.add(i).astype(self.total.dtype)
+            self.back_copy(i).start()
+
+    def back_step(self, i):
+        @pl.when(jnp.logical_not(self.last))
+        def _():
+            self.back_copy(i).wait_recv()
+
+        @pl.when(jnp.logical_not(self.first | self.last))
+        def _():
+            self.back_copy(i).start()
+
+    def finish(self, count):
+        for i in range(count):
+
+            @pl.when(jnp.logical_not(self.last))
+            def _():
+                self.out_copy(i, False).wait_send()
+
+            @pl.when(jnp.logical_not(self.first))
+            def _():
+                self.back_copy(i).wait_send()
+
+
+def chain_kernel(chain, count, lag, term, out, passing, total, sems):
+    greet_chain(chain)
+    half = term.shape[0] // 2
+    rows = half // count
+    sums = [
+        ChainSum(chain, upward, term, passing, total, first, rows, sems.at[k])
+        for k, (upward, first) in enumerate(((True, 0), (False, half)))
+    ]
+    for i in range(count + lag):
+        if i < count:
+            for part in sums:
+                part.out_step(i)
+        if i >= lag:
+            for part in sums:
+                part.back_step(i - lag)
+    for part in sums:
+        part.finish(count)
+    out[...] = total[...]
+
+
+def chain_sum(term, chain, collective_id, count=8, lag=4):
+    return pl.pallas_call(
+        functools.partial(chain_kernel, chain, count, lag),
+        out_shape=jax.ShapeDtypeStruct(term.shape, term.dtype),
+        in_specs=[pl.BlockSpec(memory_space=pltpu.VMEM)],
+        out_specs=pl.BlockSpec(memory_space=pltpu.VMEM),
+        scratch_shapes=[
+            pltpu.VMEM(term.shape, term.dtype),
+            pltpu.VMEM(term.shape, term.dtype),
+            pltpu.SemaphoreType.DMA((2, 4, count)),
+        ],
+        compiler_params=pltpu.CompilerParams(
+            collective_id=collective_id, has_side_effects=True, vmem_limit_bytes=VMEM_BYTES
+        ),
+        name="chain_sum",
+    )(term)
+
+
+class Scatter:
+    COPIES = 10
+
+    def __init__(self, grad, axis, own, sib, near, sems, local):
+        self.grad, self.axis, self.own, self.sib, self.near = grad, axis, own, sib, near
+        self.sems, self.local = sems, local
+        self.me = lax.axis_index("tokens")
+
+    def sib_copy(self, k):
+        index = jnp.bitwise_xor(self.me, 2 * k + 1)
+        return remote(
+            block_of(self.grad, self.axis, index),
+            self.sib.at[k],
+            self.sems.at[0, k],
+            self.sems.at[1, k],
+            token_device(1),
+        )
+
+    def own_copy(self, k):
+        index = jnp.bitwise_xor(self.me, 2 * k)
+        return pltpu.make_async_copy(
+            block_of(self.grad, self.axis, index), self.own.at[k], self.local.at[k]
+        )
+
+    def half(self, ref, k, half):
+        rows = ref.shape[1] // 2
+        return ref.at[k, pl.ds(half * rows, rows)]
+
+    def chip_copy(self, slot):
+        k, half, flip = ((1, 0, 2), (3, 0, 2), (2, 1, 4), (3, 1, 4), (2, 0, 4), (1, 1, 2))[slot]
+        return remote(
+            self.half(self.own, k, half),
+            self.near.at[slot],
+            self.sems.at[0, 4 + slot],
+            self.sems.at[1, 4 + slot],
+            token_device(flip),
+        )
+
+    def start(self):
+        for k in (3, 1, 2, 0):
+            self.sib_copy(k).start()
+            self.own_copy(k).start()
+
+    def cores(self):
+        for k in (3, 1, 2, 0):
+            self.sib_copy(k).wait_recv()
+            self.own_copy(k).wait()
+            self.own[k] = (
+                self.own[k].astype(jnp.float32) + self.sib[k].astype(jnp.float32)
+            ).astype(self.own.dtype)
+            for slot in {3: (1, 3), 1: (0,), 2: (2,), 0: ()}[k]:
+                self.chip_copy(slot).start()
+
+    def add_near(self, k, half, slot):
+        rows = self.own.shape[1] // 2
+        place = pl.ds(half * rows, rows)
+        self.own[k, place] = (
+            self.own[k, place].astype(jnp.float32) + self.near[slot].astype(jnp.float32)
+        ).astype(self.own.dtype)
+
+    def second(self):
+        self.chip_copy(1).wait_recv()
+        self.add_near(2, 0, 1)
+        self.chip_copy(4).start()
+        self.chip_copy(3).wait_recv()
+        self.add_near(1, 1, 3)
+        self.chip_copy(5).start()
+
+    def finish(self, out):
+        rows = self.own.shape[1] // 2
+        for half, slots in ((0, (0, 4)), (1, (2, 5))):
+            place = pl.ds(half * rows, rows)
+            total = self.own[0, place].astype(jnp.float32)
+            for slot in slots:
+                self.chip_copy(slot).wait_recv()
+                total = total + self.near[slot].astype(jnp.float32)
+            out[place, :] = total
+        for k in range(4):
+            self.sib_copy(k).wait_send()
+        for slot in range(6):
+            self.chip_copy(slot).wait_send()
+
+
+def scatter_kernel(axes, *refs):
+    count = len(axes)
+    grads, outs = refs[:count], refs[count : 2 * count]
+    owns = refs[2 * count : 3 * count]
+    sibs = refs[3 * count : 4 * count]
+    nears = refs[4 * count : 5 * count]
+    sems, local = refs[5 * count :]
+    greet_cube()
+    parts = [
+        Scatter(grads[i], axes[i], owns[i], sibs[i], nears[i], sems.at[i], local.at[i])
+        for i in range(count)
+    ]
+    for i in range(count + 2):
+        if i < count:
+            parts[i].start()
+        if 0 <= i - 1 < count:
+            parts[i - 1].cores()
+        if 0 <= i - 2 < count:
+            parts[i - 2].second()
+    for part, out in zip(parts, outs):
+        part.finish(out)
+
+
+def scatter_sums(arrays, axes, collective_id):
+    count = len(arrays)
+    blocks = [
+        tuple(size // 8 if d == axis else size for d, size in enumerate(array.shape))
+        for array, axis in zip(arrays, axes)
+    ]
+    return pl.pallas_call(
+        functools.partial(scatter_kernel, axes),
+        out_shape=[jax.ShapeDtypeStruct(s, jnp.float32) for s in blocks],
+        in_specs=[pl.BlockSpec(memory_space=pl.ANY)] * count,
+        out_specs=[pl.BlockSpec(memory_space=pltpu.VMEM)] * count,
+        scratch_shapes=[pltpu.VMEM((4,) + s, a.dtype) for s, a in zip(blocks, arrays)]
+        + [pltpu.VMEM((4,) + s, a.dtype) for s, a in zip(blocks, arrays)]
+        + [pltpu.VMEM((6, s[0] // 2, s[1]), a.dtype) for s, a in zip(blocks, arrays)]
+        + [
+            pltpu.SemaphoreType.DMA((count, 2, Scatter.COPIES)),
+            pltpu.SemaphoreType.DMA((count, 4)),
+        ],
+        compiler_params=pltpu.CompilerParams(
+            collective_id=collective_id, has_side_effects=True, vmem_limit_bytes=VMEM_BYTES
+        ),
+        name="scatter_sums",
+    )(*arrays)
+
+
+def shards_cube(
+    chain,
+    inputs,
+    segments,
+    pre_gain,
+    mid_gain,
+    query_weight,
+    key_weight,
+    value_weight,
+    out_weight,
+    gate_weight,
+    up_weight,
+    down_weight,
+    cotangent,
+):
+    row_count = inputs.shape[0]
+    head_size = key_weight.shape[1]
+    heads_here = query_weight.shape[1] // head_size
+    myself = lax.axis_index("tokens")
+    small = jnp.stack(
+        [
+            segments.astype(jnp.float32),
+            jnp.concatenate([pre_gain, mid_gain]).astype(jnp.float32),
+        ]
+    )
+    small = jnp.concatenate([small, jnp.zeros((14, row_count), jnp.float32)])
+    in_weight = jnp.concatenate([query_weight, key_weight, value_weight], axis=1)
+    small_full, in_full, out_full, gate_full, up_full, down_full = gather_weights(
+        (small, in_weight, out_weight, gate_weight, up_weight, down_weight), (0, 0, 1, 0, 0, 1), 0
+    )
+    query_width = query_weight.shape[1]
+    query_full = in_full[:, :query_width]
+    key_full = in_full[:, query_width : query_width + head_size]
+    value_full = in_full[:, query_width + head_size :]
+    small_full = small_full.reshape(8, 16, row_count)
+    all_ids = small_full[:, 0].reshape(-1).astype(jnp.int32)
+    pre_row = small_full[:, 1, : row_count // 2].reshape(-1)
+    mid_row = small_full[:, 1, row_count // 2 :].reshape(-1)
+    length = all_ids.shape[0]
+    places = jnp.arange(length, dtype=jnp.int32)
+    starts_here = jnp.concatenate([jnp.ones((1,), dtype=jnp.bool_), all_ids[1:] != all_ids[:-1]])
+    opening = lax.cummax(jnp.where(starts_here, places, 0), axis=0)
+    own_first = myself * row_count
+    positions = lax.dynamic_slice_in_dim(places - opening, own_first, row_count)
+    own_places = own_first + jnp.arange(row_count, dtype=jnp.int32)
+    half_size = head_size // 2
+    inverse = 10000.0 ** (-jnp.arange(half_size, dtype=jnp.float32) / half_size)
+    turned = positions.astype(jnp.float32)[:, None] * inverse[None, :]
+    cos_table = jnp.cos(turned)[:, None, :]
+    sin_table = jnp.sin(turned)[:, None, :]
+    inputs_f = inputs.astype(jnp.float32)
+    pre_scale = rms_scale(inputs_f)
+    normed = (inputs_f * pre_scale * pre_row).astype(jnp.bfloat16)
+    queries = jnp.dot(normed, query_full, preferred_element_type=jnp.float32).reshape(
+        row_count, heads_here, head_size
+    )
+    query_rot = (rotate(queries, cos_table, sin_table) * head_size ** (-0.5)).astype(jnp.bfloat16)
+    key_rows = jnp.dot(normed, key_full, preferred_element_type=jnp.float32)[:, None, :]
+    key_rot = rotate(key_rows, cos_table, sin_table)[:, 0, :].astype(jnp.bfloat16)
+    value_low = jnp.dot(normed, value_full, preferred_element_type=jnp.float32).astype(jnp.bfloat16)
+    key_all, value_all = (
+        lax.all_gather(key_rot, "tokens", axis=0, tiled=True),
+        lax.all_gather(value_low, "tokens", axis=0, tiled=True),
+    )
+    span = math.gcd(ROW, 1024)
+    row_start = own_first // ROW * ROW
+    block_first = row_start // span
+    block_total = (own_first + row_count + span - 1) // span
+
+    def key_block(block_index):
+        opening_row = block_index * span
+        block_keys = lax.dynamic_slice_in_dim(key_all, opening_row, span)
+        block_values = lax.dynamic_slice_in_dim(value_all, opening_row, span)
+        block_ids = lax.dynamic_slice_in_dim(all_ids, opening_row, span)
+        block_places = opening_row + jnp.arange(span, dtype=jnp.int32)
+        allowed = (segments[:, None] == block_ids[None, :]) & (
+            own_places[:, None] >= block_places[None, :]
+        )
+        scores = jnp.einsum(
+            "qhd,kd->qhk", query_rot, block_keys, preferred_element_type=jnp.float32
+        )
+        return (opening_row, block_keys, block_values, allowed[:, None, :], scores)
+
+    def forward_step(block_index, state_now):
+        row_peak, row_total, running = state_now
+        opening_row, block_keys, block_values, allowed, scores = key_block(block_index)
+        new_peak = jnp.maximum(row_peak, jnp.max(jnp.where(allowed, scores, -1e30), axis=-1))
+        factor = jnp.exp(row_peak - new_peak)
+        weights = jnp.where(allowed, jnp.exp(scores - new_peak[..., None]), 0.0)
+        row_total = row_total * factor + jnp.sum(weights, axis=-1)
+        running = running * factor[..., None] + jnp.einsum(
+            "qhk,kd->qhd",
+            weights.astype(jnp.bfloat16),
+            block_values,
+            preferred_element_type=jnp.float32,
+        )
+        return (new_peak, row_total, running)
+
+    start_state = (
+        jnp.full((row_count, heads_here), -1e30, jnp.float32),
+        jnp.zeros((row_count, heads_here), jnp.float32),
+        jnp.zeros((row_count, heads_here, head_size), jnp.float32),
+    )
+    row_peak, row_total, running = lax.fori_loop(
+        block_first, block_total, forward_step, start_state
+    )
+    attended = running / row_total[..., None]
+    log_total = row_peak + jnp.log(row_total)
+    attended_low = attended.astype(jnp.bfloat16).reshape(row_count, heads_here * head_size)
+    attn_term = jnp.dot(attended_low, out_full, preferred_element_type=jnp.float32)
+    middle = inputs_f + chain_sum(attn_term.astype(jnp.bfloat16), chain, 1).astype(jnp.float32)
+    mid_scale = rms_scale(middle)
+    normed_mid = (middle * mid_scale * mid_row).astype(jnp.bfloat16)
+    gate_rows = jnp.dot(normed_mid, gate_full, preferred_element_type=jnp.float32)
+    up_rows = jnp.dot(normed_mid, up_full, preferred_element_type=jnp.float32)
+    sigmoid_rows = jax.nn.sigmoid(gate_rows)
+    silu_rows = gate_rows * sigmoid_rows
+    hidden = (silu_rows * up_rows).astype(jnp.bfloat16)
+    mlp_term = jnp.dot(hidden, down_full, preferred_element_type=jnp.float32)
+    layer_out = (
+        middle + chain_sum(mlp_term.astype(jnp.bfloat16), chain, 2).astype(jnp.float32)
+    ).astype(jnp.bfloat16)
+    grad_down = jnp.einsum("tf,td->fd", hidden, cotangent, preferred_element_type=jnp.float32)
+    back_hidden = jnp.einsum("td,fd->tf", cotangent, down_full, preferred_element_type=jnp.float32)
+    back_gate = (
+        back_hidden * up_rows * sigmoid_rows * (1.0 + gate_rows * (1.0 - sigmoid_rows))
+    ).astype(jnp.bfloat16)
+    back_up = (back_hidden * silu_rows).astype(jnp.bfloat16)
+    grad_gate = jnp.einsum("tc,tf->cf", normed_mid, back_gate, preferred_element_type=jnp.float32)
+    grad_up = jnp.einsum("tc,tf->cf", normed_mid, back_up, preferred_element_type=jnp.float32)
+    mid_term = jnp.einsum(
+        "tf,cf->tc", back_gate, gate_full, preferred_element_type=jnp.float32
+    ) + jnp.einsum("tf,cf->tc", back_up, up_full, preferred_element_type=jnp.float32)
+    back_normed_mid = chain_sum(mid_term.astype(jnp.bfloat16), chain, 3).astype(jnp.float32)
+    back_middle, grad_mid = norm_back(back_normed_mid, middle, mid_scale, mid_row)
+    back_middle = back_middle + cotangent.astype(jnp.float32)
+    back_attn = back_middle.astype(jnp.bfloat16)
+    grad_out = jnp.einsum("tc,td->cd", attended_low, back_attn, preferred_element_type=jnp.float32)
+    back_attended = (
+        jnp.einsum("td,cd->tc", back_attn, out_full, preferred_element_type=jnp.float32)
+        .astype(jnp.bfloat16)
+        .reshape(row_count, heads_here, head_size)
+    )
+    row_delta = jnp.sum(back_attended.astype(jnp.float32) * attended, axis=-1)
+
+    def backward_step(block_index, state_now):
+        back_rows, back_pairs = state_now
+        opening_row, block_keys, block_values, allowed, scores = key_block(block_index)
+        chances = jnp.where(allowed, jnp.exp(scores - log_total[..., None]), 0.0)
+        back_values = jnp.einsum(
+            "qhk,qhd->kd",
+            chances.astype(jnp.bfloat16),
+            back_attended,
+            preferred_element_type=jnp.float32,
+        )
+        back_chances = jnp.einsum(
+            "qhd,kd->qhk", back_attended, block_values, preferred_element_type=jnp.float32
+        )
+        back_scores = (chances * (back_chances - row_delta[..., None])).astype(jnp.bfloat16)
+        back_rows = back_rows + jnp.einsum(
+            "qhk,kd->qhd", back_scores, block_keys, preferred_element_type=jnp.float32
+        )
+        back_keys = jnp.einsum(
+            "qhk,qhd->kd", back_scores, query_rot, preferred_element_type=jnp.float32
+        )
+        old_piece = lax.dynamic_slice_in_dim(back_pairs, opening_row, span)
+        fresh_piece = old_piece + jnp.concatenate([back_keys, back_values], axis=-1)
+        back_pairs = lax.dynamic_update_slice_in_dim(back_pairs, fresh_piece, opening_row, 0)
+        return (back_rows, back_pairs)
+
+    start_back = (
+        jnp.zeros((row_count, heads_here, head_size), jnp.float32),
+        jnp.zeros((length, 2 * head_size), jnp.float32),
+    )
+    back_rows, back_pairs = lax.fori_loop(block_first, block_total, backward_step, start_back)
+    own_pairs = lax.psum_scatter(
+        back_pairs.astype(jnp.bfloat16), "tokens", scatter_dimension=0, tiled=True
+    ).astype(jnp.float32)
+    back_query = (
+        (unrotate(back_rows, cos_table, sin_table) * head_size ** (-0.5))
+        .astype(jnp.bfloat16)
+        .reshape(row_count, heads_here * head_size)
+    )
+    back_key = unrotate(own_pairs[:, None, :head_size], cos_table, sin_table)[:, 0, :].astype(
+        jnp.bfloat16
+    )
+    back_value = own_pairs[:, head_size:].astype(jnp.bfloat16)
+    grad_query = jnp.einsum("tc,tq->cq", normed, back_query, preferred_element_type=jnp.float32)
+    grad_key = jnp.einsum("tc,tq->cq", normed, back_key, preferred_element_type=jnp.float32)
+    grad_value = jnp.einsum("tc,tq->cq", normed, back_value, preferred_element_type=jnp.float32)
+    pre_term = jnp.einsum("tq,cq->tc", back_query, query_full, preferred_element_type=jnp.float32)
+    pre_term = pre_term + jnp.einsum(
+        "tq,cq->tc", back_key, key_full, preferred_element_type=jnp.float32
+    )
+    pre_term = pre_term + jnp.einsum(
+        "tq,cq->tc", back_value, value_full, preferred_element_type=jnp.float32
+    )
+    back_normed = chain_sum(pre_term.astype(jnp.bfloat16), chain, 4).astype(jnp.float32)
+    back_inputs, grad_pre = norm_back(back_normed, inputs_f, pre_scale, pre_row)
+    grad_input = (back_middle + back_inputs).astype(jnp.bfloat16)
+    grad_in = jnp.concatenate([grad_query, grad_key, grad_value], axis=1).astype(jnp.bfloat16)
+    grad_gate, grad_up, grad_down, grad_in, grad_out = scatter_sums(
+        (
+            grad_gate.astype(jnp.bfloat16),
+            grad_up.astype(jnp.bfloat16),
+            grad_down.astype(jnp.bfloat16),
+            grad_in,
+            grad_out.astype(jnp.bfloat16),
+        ),
+        (0, 0, 1, 0, 1),
+        5,
+    )
+    grad_query = grad_in[:, :query_width]
+    grad_key = grad_in[:, query_width : query_width + head_size]
+    grad_value = grad_in[:, query_width + head_size :]
+    grad_pre, grad_mid = (
+        lax.psum_scatter(part.astype(jnp.bfloat16), "tokens", scatter_dimension=0, tiled=True).astype(jnp.float32)
+        for part in (grad_pre, grad_mid)
+    )
+    return (
+        layer_out,
+        grad_input,
+        grad_pre,
+        grad_mid,
+        grad_query,
+        grad_key,
+        grad_value,
+        grad_out,
+        grad_gate,
+        grad_up,
+        grad_down,
+    )
+
+
 def solution(mesh):
+    sizes = dict(mesh.shape)
+    plan = shards_any
+    if sizes["tokens"] == 8:
+        plan = functools.partial(shards_cube, sizes["heads"])
     return jax.shard_map(
-        shards,
+        plan,
         mesh=mesh,
         in_specs=(
             P("tokens", None),

time: 1100 us -> 1550 us (1.41)
  Pallas kernels: 0 us -> 1300 us
  waiting for transfers between devices: 756 us -> 0.02 us
  blocking collectives: 112 us -> 32.8 us
  matrix products: 144 us -> 123 us
    pallas_call x0 -> x6, Pallas kernels: none -> 1300 us  [the longest x4 1030 us: chain_sum(): pl.pallas_call(functools.partial(chain_kernel, chain, count, lag), out_sh...]
    psum x3 -> x0, waiting for transfers between devices: 320 us -> none  [the longest x1 157 us: shards(): lax.psum(mlp_term.astype(jnp.bfloat16), 'heads').astype(jnp.float32)]
    reduce_scatter x8 -> x1, waiting for transfers between devices: 319 us -> 0.01 us  [shards_cube(): lax.psum_scatter(back_pairs.astype(jnp.bfloat16), 'tokens', scatter_dimen...]
    all_gather x5 -> x0, waiting for transfers between devices: 114 us -> none  [the longest x1 39.3 us: shards(): lax.all_gather(up_weight, 'tokens', axis=0, tiled=True)]
    all_gather x7 -> x2, blocking collectives: 97.6 us -> 20.8 us  [the longest x1 10.4 us: shards_cube(): lax.all_gather(key_rot, 'tokens', axis=0, tiled=True)]
    dot_general x21, matrix products: 102 us -> 83.3 us  [the longest x1 7.37 us: shards_cube(): mlp_term = jnp.dot(hidden, down_full, preferred_element_type=jnp.float32)]
  transfers between devices with their start and end apart: 16 -> 1, of which waited for: 13 -> 0; matrix products, arithmetic and copies ran while one was open for 13% -> 2% of each run, Pallas kernels for 0% -> 16%
where the time goes in v1:
time: 1550 us; the launch traced here: 1540 us
  Pallas kernels  1300 us (84%)
  matrix products  123 us (8%)
  other arithmetic  47.6 us (3%)
  blocking collectives  32.8 us (2%)
  local copies, waits for them, and re-layouts  17.1 us (1%)
  between operations  15.9 us (1%)
    pallas_call x4, Pallas kernels, chain_sum(): pl.pallas_call(functools.partial(chain_kernel, chain, count, lag), out_sh...  1030 us
    pallas_call x1, Pallas kernels, scatter_sums(): pl.pallas_call(functools.partial(scatter_kernel, axes), out_shape=[jax.Sh...  150 us
    pallas_call x1, Pallas kernels, gather_weights(): pl.pallas_call(functools.partial(gather_kernel, axes), out_shape=[jax.Sha...  123 us
  transfers between devices with their start and end apart: 1, of which 0 were waited for; matrix products, arithmetic and copies ran while one was open for 2% of the time, Pallas kernels for 16%

profile of v1, /device:TPU:0, one launch (start us, length us, event | category | flops | bytes accessed | tf_op | source)
XLA Modules:
  0.0 1541.8 jit_solution(10817405728990982449)
XLA Ops:
  11.9 1.8 pad_maximum_fusion.1.refs_1_
  13.7 122.5 %gather_weights.1 = (f32[128,512]{1,0:T(8,128)}, bf16[2048,640]{1,0:T(8,128)(2,1)}, bf16[512,2048]{1,0:T(8,128)(2,1)}, bf16[2048,1408]{1,0:T(8,128)(2,1)}, bf16[...) custom-call(f32[16,512]{1,0:T(8,128)} %maximum_maximum_fusion.refs_0_, bf16[256,640]{1,0:T(8,128)(2,1)} %pad_maximum_fusion.1.refs_1_, ...), custom_call_target="tpu_custom_call" | custom-call | tf_op jit(solution)/shard_map/gather_weights/pallas_call | solution.py:427
  138.8 2.0 convolution_convert_fusion.10
  141.7 1.4 fusion.65
  144.7 10.4 all_gather.7
  155.0 10.4 all-gather
  166.9 28.9 %while.28 = (s32[]{:T(128)}, f32[512,8]{0,1:T(8,128)S(1)}, f32[512,8]{0,1:T(8,128)S(1)}, f32[512,8,64]{0,2,1:T(8,128)}, s32[]{:T(128)}, /*index=5*/s32[512]{0:T(...) while((s32[]{:T(128)}, f32[512,8]{0,1:T(8,128)S(1)}, ...), condition=%wide.region_6.7_spmd.clone, body=%wide.region_3.6_spmd.clone.sunk | while | flops 1109403136 | bytes 55601356 | solution.py:815
  168.0 9.2 fusion.166
  177.2 8.6 fusion.167
  185.9 9.9 fusion.168
  195.8 1.3 fusion.76
  197.2 4.4 convolution_convert_fusion.5.term
  201.6 260.9 %chain_sum.4 = bf16[512,2048]{1,0:T(8,128)(2,1)} custom-call(bf16[512,2048]{1,0:T(8,128)(2,1)} %convolution_convert_fusion.5.term), custom_call_target="tpu_custom_call" | custom-call | tf_op jit(solution)/shard_map/chain_sum/pallas_call | solution.py:564
  462.5 2.5 multiply_reduce_fusion
  466.2 6.6 fusion.110
  472.9 3.4 fusion.109
  476.3 5.6 multiply_convert_fusion.1
  482.0 3.4 fusion.111
  485.5 4.7 add_convert_fusion.1.term
  490.1 257.7 %chain_sum.6 = bf16[512,2048]{1,0:T(8,128)(2,1)} custom-call(bf16[512,2048]{1,0:T(8,128)(2,1)} %add_convert_fusion.1.term), custom_call_target="tpu_custom_call" | custom-call | tf_op jit(solution)/shard_map/chain_sum/pallas_call | solution.py:564
  747.9 4.5 fusion.56
  752.5 5.2 multiply_reduce_fusion.1
  757.8 1.5 broadcast_in_dim.79
  759.3 24.0 %while.29 = (s32[]{:T(128)}, f32[512,8,64]{0,2,1:T(8,128)S(1)}, f32[4096,128]{0,1:T(8,128)}, s32[]{:T(128)}, s32[512]{0:T(512)S(1)}, /*index=5*/s32[4096]{0:T(10...) while((s32[]{:T(128)}, f32[512,8,64]{0,2,1:T(8,128)S(1)}, ...), condition=%wide.region_11.12_spmd.clone, body=%wide.region_10.11_spmd.clone.sunk | while | flops 2720007680 | bytes 119482656 | solution.py:886
  760.2 2.4 fusion.179
  762.6 3.0 fusion.181
  765.6 7.6 fusion.180
  773.2 6.2 convolution_bitcast_fusion.4
  779.3 1.7 convolution_add_fusion.2
  781.0 1.9 fusion.182
  783.3 2.8 convert_element_type.173
  786.2 7.4 convolution_convert_fusion.6.term
  793.6 5.0 convolution_convert_fusion.refs_2_
  798.6 5.3 convolution_convert_fusion.1.refs_1_
  803.9 251.8 %chain_sum.5 = bf16[512,2048]{1,0:T(8,128)(2,1)} custom-call(bf16[512,2048]{1,0:T(8,128)(2,1)} %convolution_convert_fusion.6.term), custom_call_target="tpu_custom_call" | custom-call | tf_op jit(solution)/shard_map/chain_sum/pallas_call | solution.py:564
  1056.0 5.0 fusion.63
  1062.4 2.8 convolution_convert_fusion.4
  1065.2 5.4 convolution_convert_fusion.2.refs_0_
  1070.8 3.6 convolution_convert_fusion.3.refs_4_
  1076.3 3.8 fusion.73
  1081.5 3.4 pad_maximum_fusion.refs_3_
  1084.9 149.9 %scatter_sums.1 = (f32[256,1408]{1,0:T(8,128)}, f32[256,1408]{1,0:T(8,128)}, f32[1408,256]{1,0:T(8,128)}, f32[256,640]{1,0:T(8,128)}, f32[512,256]{1,0:T(8,128)}) custom-call(bf16[2048,1408]{1,0:T(8,128)(2,1)} %convolution_convert_fusion.2.refs_0_, bf16[2048,1408]{1,0:T(8,128)(2,1)} %convolution_convert_fusion.1.refs_1_, ...), custom_call_target="tpu_custom_call" | custom-call | tf_op jit(solution)/shard_map/scatter_sums/pallas_call | solution.py:693
  1235.9 1.9 slice.92
  1237.8 5.8 add_convert_fusion.term
  1243.6 261.8 %chain_sum.7 = bf16[512,2048]{1,0:T(8,128)(2,1)} custom-call(bf16[512,2048]{1,0:T(8,128)(2,1)} %add_convert_fusion.term), custom_call_target="tpu_custom_call" | custom-call | tf_op jit(solution)/shard_map/chain_sum/pallas_call | solution.py:564
  1505.4 2.9 fusion.59
  1509.7 12.0 all-reduce.2
  1521.8 8.2 fusion.52
  (191 shorter events, 25.6 us)
Async XLA Ops:
  7.2 131.1 %copy-start.1 = (bf16[512,2048]{1,0:T(8,128)(2,1)S(1)}, bf16[512,2048]{1,0:T(8,128)(2,1)}, u32[]{:S(2)}) copy-start(bf16[512,2048]{1,0:T(8,128)(2,1)} %param.16) | copy-start | bytes 6291460
  7.2 1067.1 %reduce-scatter.2.cloned.1.call-start = ((), (), s32[]{:S(2)}) async-start(), calls=%async_computation.1 | async-start | bytes 1179648 | tf_op jit(solution)/shard_map/reduce_scatter | solution.py:887
  7.3 137.0 %copy-start.46 = (f32[32]{0:T(128)}, f32[32]{0:T(128)S(1)}, u32[]{:S(2)}) copy-start(f32[32]{0:T(128)S(1)} %multiply_power_fusion) | copy-start | bytes 388
  136.3 4.5 copy-start.13
  138.2 614.2 %copy-start.29 = (f32[8,1,256]{2,1,0:T(1,128)}, f32[8,1,256]{2,1,0:T(1,128)S(1)}, u32[]{:S(2)}) copy-start(f32[8,1,256]{2,1,0:T(1,128)S(1)} %get-tuple-element.336) | copy-start | bytes 24580
  143.1 23.8 %copy-start.28 = (s32[512]{0:T(512)S(1)}, s32[512]{0:T(512)}, u32[]{:S(2)}) copy-start(s32[512]{0:T(512)} %param.17) | copy-start | bytes 6148
  144.0 11.0 copy-start.37
  144.3 21.4 %copy-start.20 = (f32[512,32]{0,1:T(8,128)}, f32[512,32]{0,1:T(8,128)S(1)}, u32[]{:S(2)}) copy-start(f32[512,32]{0,1:T(8,128)S(1)} %get-tuple-element.342) | copy-start | bytes 196612
  144.3 22.6 %copy-start.22 = (f32[512,32]{0,1:T(8,128)}, f32[512,32]{0,1:T(8,128)S(1)}, u32[]{:S(2)}) copy-start(f32[512,32]{0,1:T(8,128)S(1)} %get-tuple-element.343) | copy-start | bytes 196612
  197.2 265.3 %copy-start.24 = (bf16[512,8,64]{0,2,1:T(8,128)(2,1)}, bf16[512,8,64]{0,2,1:T(8,128)(2,1)S(1)}, u32[]{:S(2)}) copy-start(bf16[512,8,64]{0,2,1:T(8,128)(2,1)S(1)} %fusion.76) | copy-start | bytes 1572868
  465.0 287.5 %copy-start.34 = (f32[512]{0:T(512)}, f32[512]{0:T(512)S(1)}, u32[]{:S(2)}) copy-start(f32[512]{0:T(512)S(1)} %add_rsqrt_fusion) | copy-start | bytes 6148
  465.0 7.8 slice-start.4
  466.2 6.6 copy-start.14
  466.2 6.6 slice-start.5
  466.2 10.1 slice-start
  472.9 12.6 slice-start.2
  476.3 9.1 slice-start.3
  747.9 4.6 copy-start.4
  747.9 4.6 copy-start.6
  747.9 4.6 copy-start.7
  752.5 5.2 copy-start.42
  752.5 6.8 copy-start.9
  773.2 6.2 copy-start
  786.2 7.4 copy-start.11
  793.6 5.0 copy-start.15
  793.6 5.0 copy-start.53
  803.9 251.8 %copy-start.21 = (f32[512,32]{0,1:T(8,128)S(1)}, f32[512,32]{0,1:T(8,128)}, u32[]{:S(2)}) copy-start(f32[512,32]{0,1:T(8,128)} %copy-done.20) | copy-start | bytes 196612
  803.9 251.8 %copy-start.23 = (f32[512,32]{0,1:T(8,128)S(1)}, f32[512,32]{0,1:T(8,128)}, u32[]{:S(2)}) copy-start(f32[512,32]{0,1:T(8,128)} %copy-done.22) | copy-start | bytes 196612
  1056.0 5.1 copy-start.48
  1056.0 6.3 copy-start.2
  1056.0 6.3 copy-start.33
  1056.0 6.3 copy-start.40
  1065.2 5.5 copy-start.5
  1065.2 5.5 copy-start.8
  1065.2 5.5 copy-start.12
  1065.2 5.5 copy-start.25
  1065.2 5.5 copy-start.30
  1065.2 5.5 copy-start.35
  1065.2 5.5 copy-start.43
  1070.7 4.4 copy-start.38
  1070.7 4.4 copy-start.47
  1075.5 4.9 copy-start.31
  1243.5 261.8 %copy-start.41 = (f32[512]{0:T(512)S(1)}, f32[512]{0:T(512)}, u32[]{:S(2)}) copy-start(f32[512]{0:T(512)} %copy-done.39) | copy-start | bytes 6148
  1243.5 266.2 %copy-start.45 = (bf16[2048]{0:T(1024)(128)(2,1)S(1)}, bf16[2048]{0:T(1024)(128)(2,1)}, u32[]{:S(2)}) copy-start(bf16[2048]{0:T(1024)(128)(2,1)} %get-tuple-element.267) | copy-start | bytes 12292
  1243.6 278.2 %copy-start.36 = (f32[512]{0:T(512)S(1)}, f32[512]{0:T(512)}, u32[]{:S(2)}) copy-start(f32[512]{0:T(512)} %copy-done.34) | copy-start | bytes 6148
  1243.6 278.2 %copy-start.44 = (f32[512]{0:T(512)S(1)}, f32[512]{0:T(512)}, u32[]{:S(2)}) copy-start(f32[512]{0:T(512)} %copy-done.42) | copy-start | bytes 6148
  1521.8 8.8 copy-start.27
  1521.8 9.6 copy-start.19
  (13 other events, 39.9 us)
Sparse Core Ops, SparseCore 0:
  786.3 89.7 reduce-scatter.1

commit v2 on v1

--- a/solution.py
+++ b/solution.py
@@ -339,8 +339,9 @@
 class Gather:
     COPIES = 9
 
-    def __init__(self, shard, full, axis, send, recv):
-        self.shard, self.full, self.axis, self.send, self.recv = shard, full, axis, send, recv
+    def __init__(self, shard, full, axis, send, recv, local):
+        self.shard, self.full, self.axis = shard, full, axis
+        self.send, self.recv, self.local = send, recv, local
         self.me = lax.axis_index("tokens")
 
     def copy(self, slot, flip_block, flip_target, half=None):
@@ -370,12 +371,15 @@
             )[slot],
         )
 
-    def start(self, local):
+    def own_copy(self):
+        return pltpu.make_async_copy(
+            self.shard, block_of(self.full, self.axis, self.me), self.local
+        )
+
+    def start(self):
         for slot in (0, 1, 2):
             self.copies(slot).start()
-        mine = pltpu.make_async_copy(self.shard, block_of(self.full, self.axis, self.me), local)
-        mine.start()
-        mine.wait()
+        self.own_copy().start()
 
     def relay(self):
         self.copies(0).wait_recv()
@@ -396,47 +400,7 @@
             self.copies(slot).wait_recv()
         for slot in range(self.COPIES):
             self.copies(slot).wait_send()
-
-
-def gather_kernel(axes, *refs):
-    count = len(axes)
-    shards_in, fulls = refs[:count], refs[count : 2 * count]
-    send, recv, local = refs[2 * count :]
-    greet_cube()
-    parts = [
-        Gather(shards_in[i], fulls[i], axes[i], send.at[i], recv.at[i]) for i in range(count)
-    ]
-    ahead = 2
-    for i in range(count + ahead + 1):
-        if i < count:
-            parts[i].start(local.at[i])
-        if 0 <= i - ahead < count:
-            parts[i - ahead].relay()
-        if 0 <= i - ahead - 1 < count:
-            parts[i - ahead - 1].finish_relay()
-    for part in parts:
-        part.finish()
-
-
-def gather_weights(arrays, axes, collective_id):
-    count = len(arrays)
-    shapes = [
-        tuple(size * 8 if d == axis else size for d, size in enumerate(array.shape))
-        for array, axis in zip(arrays, axes)
-    ]
-    return pl.pallas_call(
-        functools.partial(gather_kernel, axes),
-        out_shape=[jax.ShapeDtypeStruct(s, a.dtype) for s, a in zip(shapes, arrays)],
-        in_specs=[pl.BlockSpec(memory_space=pl.ANY)] * count,
-        out_specs=[pl.BlockSpec(memory_space=pl.ANY)] * count,
-        scratch_shapes=[
-            pltpu.SemaphoreType.DMA((count, Gather.COPIES)),
-            pltpu.SemaphoreType.DMA((count, Gather.COPIES)),
-            pltpu.SemaphoreType.DMA((count,)),
-        ],
-        compiler_params=pltpu.CompilerParams(collective_id=collective_id, has_side_effects=True),
-        name="gather_weights",
-    )(*arrays)
+        self.own_copy().wait()
 
 
 def greet_chain(chain):
@@ -466,116 +430,448 @@
 
 
 class ChainSum:
-    def __init__(self, chain, upward, term, passing, total, first_row, rows, sems):
+    def __init__(self, chain, upward, term, passing, total, base, count, sems):
         self.chain, self.term, self.passing, self.total = chain, term, passing, total
-        self.first_row, self.rows = first_row, rows
+        self.base, self.count = base, count
         here = lax.axis_index("heads")
         self.rank = here if upward else chain - 1 - here
         move = 1 if upward else -1
-        clip = lambda h: jnp.clip(h, 0, chain - 1)
         tokens = lax.axis_index("tokens")
-        self.ahead = (tokens, clip(here + move))
-        self.behind = (tokens, clip(here - move))
+        self.ahead = (tokens, jnp.clip(here + move, 0, chain - 1))
+        self.behind = (tokens, jnp.clip(here - move, 0, chain - 1))
         self.sems = sems
         self.first = self.rank == 0
         self.last = self.rank == chain - 1
 
-    def place(self, i):
-        return pl.ds(self.first_row + i * self.rows, self.rows)
-
     def out_copy(self, i, first):
-        place = self.place(i)
         src = self.term if first else self.passing
+        at = self.base + i
         return remote(
-            src.at[place], self.passing.at[place], self.sems.at[0, i], self.sems.at[1, i], self.ahead
+            src.at[at], self.passing.at[at], self.sems.at[0, i], self.sems.at[1, i], self.ahead
         )
 
     def back_copy(self, i):
-        place = self.place(i)
+        at = self.base + i
         return remote(
-            self.total.at[place], self.total.at[place], self.sems.at[2, i], self.sems.at[3, i], self.behind
+            self.total.at[at], self.total.at[at], self.sems.at[2, i], self.sems.at[3, i], self.behind
         )
 
     def add(self, i):
-        place = self.place(i)
-        return self.term[place, :].astype(jnp.float32) + self.passing[place, :].astype(jnp.float32)
-
-    def out_step(self, i):
-        @pl.when(self.first)
+        at = self.base + i
+        return self.term[at].astype(jnp.float32) + self.passing[at].astype(jnp.float32)
+
+    def step(self, now):
+        i = now - self.rank
+        valid = (i >= 0) & (i < self.count)
+
+        @pl.when(valid & self.first)
         def _():
             self.out_copy(i, True).start()
 
+        @pl.when(valid & jnp.logical_not(self.first))
+        def _():
+            self.out_copy(i, False).wait_recv()
+
+        @pl.when(valid & jnp.logical_not(self.first | self.last))
+        def _():
+            self.passing[self.base + i] = self.add(i).astype(self.passing.dtype)
+            self.out_copy(i, False).start()
+
+        @pl.when(valid & self.last)
+        def _():
+            self.total[self.base + i] = self.add(i).astype(self.total.dtype)
+            self.back_copy(i).start()
+
+        j = now - (2 * (self.chain - 1) - self.rank)
+        back = (j >= 0) & (j < self.count) & jnp.logical_not(self.last)
+
+        @pl.when(back)
+        def _():
+            self.back_copy(j).wait_recv()
+
+        @pl.when(back & jnp.logical_not(self.first))
+        def _():
+            self.back_copy(j).start()
+
+    def steps(self):
+        return self.count + 2 * (self.chain - 1)
+
+    def finish(self):
+        @pl.when(jnp.logical_not(self.last))
+        def _():
+            for i in range(self.count):
+                self.out_copy(i, False).wait_send()
+
         @pl.when(jnp.logical_not(self.first))
         def _():
-            self.out_copy(i, False).wait_recv()
-
-        @pl.when(jnp.logical_not(self.first | self.last))
-        def _():
-            self.passing[self.place(i), :] = self.add(i).astype(self.passing.dtype)
-            self.out_copy(i, False).start()
-
-        @pl.when(self.last)
-        def _():
-            self.total[self.place(i), :] = self.add(i).astype(self.total.dtype)
-            self.back_copy(i).start()
-
-    def back_step(self, i):
-        @pl.when(jnp.logical_not(self.last))
-        def _():
-            self.back_copy(i).wait_recv()
-
-        @pl.when(jnp.logical_not(self.first | self.last))
-        def _():
-            self.back_copy(i).start()
-
-    def finish(self, count):
-        for i in range(count):
-
-            @pl.when(jnp.logical_not(self.last))
-            def _():
-                self.out_copy(i, False).wait_send()
-
-            @pl.when(jnp.logical_not(self.first))
-            def _():
+            for i in range(self.count):
                 self.back_copy(i).wait_send()
 
 
-def chain_kernel(chain, count, lag, term, out, passing, total, sems):
+def chain_kernel(chain, count, term, out, passing, total, sems):
     greet_chain(chain)
-    half = term.shape[0] // 2
-    rows = half // count
     sums = [
-        ChainSum(chain, upward, term, passing, total, first, rows, sems.at[k])
-        for k, (upward, first) in enumerate(((True, 0), (False, half)))
+        ChainSum(chain, upward, term, passing, total, base, count, sems.at[k])
+        for k, (upward, base) in enumerate(((True, 0), (False, count)))
     ]
-    for i in range(count + lag):
-        if i < count:
-            for part in sums:
-                part.out_step(i)
-        if i >= lag:
-            for part in sums:
-                part.back_step(i - lag)
+
+    @pl.loop(0, sums[0].steps())
+    def _(now):
+        for part in sums:
+            part.step(now)
+
     for part in sums:
-        part.finish(count)
+        part.finish()
     out[...] = total[...]
 
 
-def chain_sum(term, chain, collective_id, count=8, lag=4):
+def chain_sum(term, chain, collective_id, count=8):
+    shape = (2 * count, term.shape[0] // (2 * count), term.shape[1])
     return pl.pallas_call(
-        functools.partial(chain_kernel, chain, count, lag),
-        out_shape=jax.ShapeDtypeStruct(term.shape, term.dtype),
+        functools.partial(chain_kernel, chain, count),
+        out_shape=jax.ShapeDtypeStruct(shape, term.dtype),
         in_specs=[pl.BlockSpec(memory_space=pltpu.VMEM)],
         out_specs=pl.BlockSpec(memory_space=pltpu.VMEM),
         scratch_shapes=[
-            pltpu.VMEM(term.shape, term.dtype),
-            pltpu.VMEM(term.shape, term.dtype),
+            pltpu.VMEM(shape, term.dtype),
+            pltpu.VMEM(shape, term.dtype),
             pltpu.SemaphoreType.DMA((2, 4, count)),
         ],
         compiler_params=pltpu.CompilerParams(
             collective_id=collective_id, has_side_effects=True, vmem_limit_bytes=VMEM_BYTES
         ),
         name="chain_sum",
-    )(term)
+    )(term.reshape(shape)).reshape(term.shape)
+
+
+def lanes(shape):
+    return lax.broadcasted_iota(jnp.int32, shape, len(shape) - 1)
+
+
+def turn(vectors, cos_table, sin_table):
+    near = jnp.where(
+        lanes(vectors.shape) % 64 < 32, pltpu.roll(vectors, 96, 1), pltpu.roll(vectors, 32, 1)
+    )
+    return vectors * cos_table + near * sin_table
+
+
+def token_column(row):
+    return jnp.broadcast_to(row, (128, row.shape[1])).T
+
+
+def key_marks(column, first_id):
+    lane = lanes(column.shape) % 64
+    one_hot = (column - first_id).astype(jnp.int32) == lane
+    return jnp.where(one_hot | ((lane >= 4) & (lane < 7)), 1.0, 0.0)
+
+
+def query_marks(column, first_id):
+    lane = lanes(column.shape) % 64
+    other = (column - first_id).astype(jnp.int32) != lane
+    return jnp.where(other & (lane < 4), -1e30, 0.0)
+
+
+def nt_dot(left, right):
+    return lax.dot_general(
+        left, right, (((1,), (1,)), ((), ())), preferred_element_type=jnp.float32
+    )
+
+
+def attend_kernel(
+    chain, places, x, small, in_shard, out_shard, gate_shard, up_shard, down_shard, inverse,
+    gate_full, up_full, down_full, in_full, out_full, attn_sum, normed, query, pairs, attended, log_total,
+    cos_table, sin_table, small_all, in_here, out_here, pre_row, key_side, value_side, marks, scores, peak,
+    mixed, near_pairs, term, passing, total, small_sems, gather_sems, local_sems, pair_sems, chain_sems,
+):
+    count = term.shape[0] // 2
+    tokens = x.shape[0]
+    me = lax.axis_index("tokens")
+    place = lax.rem(me, places)
+    here = lax.axis_index("heads")
+    barrier = pltpu.get_barrier_semaphore()
+    for flip in range(1, 8):
+        pl.semaphore_signal(barrier, inc=1, device_id=token_device(flip), device_id_type=MESH_ID)
+    for step in (-1, 1):
+        near = here + step
+
+        @pl.when((near >= 0) & (near < chain))
+        def _():
+            pl.semaphore_signal(barrier, inc=1, device_id=(me, near), device_id_type=MESH_ID)
+
+    edge = (here == 0) | (here == chain - 1)
+
+    @pl.when(edge)
+    def _():
+        pl.semaphore_wait(barrier, 8)
+
+    @pl.when(jnp.logical_not(edge))
+    def _():
+        pl.semaphore_wait(barrier, 9)
+
+    def small_copy(flip):
+        return remote(
+            small,
+            small_all.at[me],
+            small_sems.at[0, flip - 1],
+            small_sems.at[1, flip - 1],
+            token_device(flip),
+        )
+
+    for flip in range(1, 8):
+        small_copy(flip).start()
+
+    def gather(k, shard, full, axis):
+        return Gather(shard, full, axis, gather_sems.at[0, k], gather_sems.at[1, k], local_sems.at[k])
+
+    gather_in = gather(0, in_shard, in_here, 0)
+    gather_out = gather(1, out_shard, out_here, 1)
+    big = [
+        gather(2, gate_shard, gate_full, 0),
+        gather(3, up_shard, up_full, 0),
+        gather(4, down_shard, down_full, 1),
+    ]
+    gather_in.start()
+    small_all[me] = small[...]
+
+    x_f = x[...].astype(jnp.float32)
+    pre_scale = lax.rsqrt(jnp.mean(x_f * x_f, axis=1, keepdims=True) + 1e-05)
+
+    for flip in range(1, 8):
+        small_copy(flip).wait_recv()
+    width = x.shape[1] // 8
+    for k in range(8):
+        pre_row[:, k * width : (k + 1) * width] = jnp.broadcast_to(
+            small_all[k, 1:2, :width], (8, width)
+        )
+    gather_in.relay()
+    gather_out.start()
+    normed[...] = (x[...].astype(jnp.float32) * pre_scale * pre_row[0:1, :]).astype(jnp.bfloat16)
+    gather_in.finish_relay()
+
+    first_device = me - place
+    first_id = (first_device // places * 4).astype(jnp.float32)
+    own = token_column(small_all[me, 0:1, :])
+    before = jnp.zeros((tokens, 1), jnp.float32)
+    for k in range(places):
+        others = small_all[first_device + k, 0:1, :]
+        before = before + jnp.sum(
+            jnp.where(others < own[:, 0:1], 1.0, 0.0), axis=1, keepdims=True
+        )
+        column = token_column(others)
+        marks[pl.ds(k * tokens, tokens), :] = key_marks(column, first_id)
+    row_index = lax.broadcasted_iota(jnp.int32, (tokens, 128), 0) + place * tokens
+    turned = (row_index.astype(jnp.float32) - before) * inverse[0:1, :]
+    cos_table[...] = jnp.cos(turned)
+    sin_signed = jnp.sin(turned)
+    sin_table[...] = jnp.where(lanes(sin_signed.shape) % 64 < 32, -sin_signed, sin_signed)
+    gather_out.relay()
+    big[0].copies(1).start()
+    gather_in.finish()
+
+    wide = in_here.shape[1]
+    heads_wide = wide - 128
+    for low in range(0, wide, 256):
+        high = min(low + 256, wide)
+        made = jnp.dot(normed[...], in_here[:, low:high], preferred_element_type=jnp.float32)
+        for group in range(low, high, 128):
+            part = made[:, group - low : group - low + 128]
+            spun = turn(part, cos_table[...], sin_table[...])
+            if group < heads_wide:
+                query[:, group : group + 128] = (spun * 0.125).astype(jnp.bfloat16)
+            else:
+                near_pairs[place] = jnp.where(lanes(part.shape) < 64, spun, part).astype(jnp.bfloat16)
+
+    def pair_copy(flip):
+        return remote(
+            near_pairs.at[place],
+            near_pairs.at[place],
+            pair_sems.at[0, flip - 1],
+            pair_sems.at[1, flip - 1],
+            token_device(flip),
+        )
+
+    for flip in range(1, places):
+        pair_copy(flip).start()
+    big[0].copies(0).start()
+    big[0].copies(2).start()
+    big[0].own_copy().start()
+    big[1].copies(1).start()
+    gather_out.finish_relay()
+    for flip in range(1, places):
+        pair_copy(flip).wait_recv()
+    big[1].copies(0).start()
+    big[1].copies(2).start()
+    big[1].own_copy().start()
+    big[2].start()
+
+    for k in range(places):
+        pair = near_pairs[k].astype(jnp.float32)
+        swapped = pltpu.roll(pair, 64, 1)
+        lane = lanes(pair.shape)
+        mark = marks[pl.ds(k * tokens, tokens), :]
+        block = pl.ds(k * tokens, tokens)
+        key_side[0, block] = jnp.where(lane < 64, pair, mark).astype(jnp.bfloat16)
+        key_side[1, block] = jnp.where(lane < 64, mark, swapped).astype(jnp.bfloat16)
+        value_side[0, block] = jnp.where(lane < 64, swapped, 1.0).astype(jnp.bfloat16)
+        value_side[1, block] = jnp.where(lane < 64, 1.0, pair).astype(jnp.bfloat16)
+        pairs[block] = near_pairs[k]
+
+    lane = lanes((tokens, 128))
+    own_marks = query_marks(own, first_id)
+
+    @pl.loop(0, query.shape[1] // 128)
+    def _(group):
+        at = pl.ds(pl.multiple_of(group * 128, 128), 128)
+        both = query[:, at].astype(jnp.float32)
+        halves = []
+        for e in range(2):
+            mine = (lane < 64) if e == 0 else (lane >= 64)
+            side = jnp.where(mine, both, own_marks).astype(jnp.bfloat16)
+
+            def look(k, masked):
+                found = nt_dot(side, key_side[e, pl.ds(pl.multiple_of(k * tokens, tokens), tokens)])
+                if masked:
+                    rows = lax.broadcasted_iota(jnp.int32, found.shape, 0)
+                    found = jnp.where(lanes(found.shape) <= rows, found, -1e30)
+                scores[k] = found
+                best = found[:, :128]
+                for part in range(128, tokens, 128):
+                    best = jnp.maximum(best, found[:, part : part + 128])
+                return best
+
+            peak[...] = look(place, True)
+
+            @pl.loop(0, place)
+            def _(k):
+                peak[...] = jnp.maximum(peak[...], look(k, False))
+
+            top = jnp.max(peak[...], axis=1, keepdims=True)
+
+            def blend(k):
+                weights = jnp.exp(scores[k] - top).astype(jnp.bfloat16)
+                return jnp.dot(
+                    weights,
+                    value_side[e, pl.ds(pl.multiple_of(k * tokens, tokens), tokens)],
+                    preferred_element_type=jnp.float32,
+                )
+
+            mixed[...] = blend(place)
+
+            @pl.loop(0, place)
+            def _(k):
+                mixed[...] += blend(k)
+
+            out = mixed[...]
+            rolled = pltpu.roll(out, 64, 1)
+            sums = jnp.where(mine, rolled, out)
+            halves.append(out / sums)
+            log_total[...] = jnp.where(
+                lane == 2 * group + e, top + jnp.log(sums), log_total[...]
+            )
+        attended[:, at] = jnp.where(lane < 64, halves[0], halves[1])
+
+    gather_out.finish()
+    low = attended[...].astype(jnp.bfloat16)
+    each = term.shape[2]
+    for k in range(0, 2 * count, 2):
+        made = jnp.dot(
+            low, out_here[:, k * each : (k + 2) * each], preferred_element_type=jnp.float32
+        ).astype(jnp.bfloat16)
+        term[k] = made[:, :each]
+        term[k + 1] = made[:, each:]
+    in_out = [
+        pltpu.make_async_copy(in_here, in_full, local_sems.at[5]),
+        pltpu.make_async_copy(out_here, out_full, local_sems.at[6]),
+    ]
+    for copy in in_out:
+        copy.start()
+    sums = [
+        ChainSum(chain, upward, term, passing, total, base, count, chain_sems.at[k])
+        for k, (upward, base) in enumerate(((True, 0), (False, count)))
+    ]
+    steps = sums[0].steps()
+    stops = [0, steps // 4, steps // 2, steps * 3 // 4, steps]
+    work = [big[0].relay, big[1].relay, big[0].finish_relay, lambda: None]
+    for begin, end, job in zip(stops[:-1], stops[1:], work):
+
+        @pl.loop(begin, end)
+        def _(now):
+            for part in sums:
+                part.step(now)
+
+        job()
+    big[2].relay()
+    big[1].finish_relay()
+    attn_sum[...] = total[...]
+    big[2].finish_relay()
+    for part in sums:
+        part.finish()
+    for part in big:
+        part.finish()
+    for copy in in_out:
+        copy.wait()
+    for flip in range(1, 8):
+        small_copy(flip).wait_send()
+    for flip in range(1, places):
+        pair_copy(flip).wait_send()
+
+
+def attend(chain, places, x, small, in_weight, out_weight, gate_weight, up_weight, down_weight, inverse):
+    tokens, width = x.shape
+    count = 8
+    wide = in_weight.shape[1]
+    heads_wide = wide - 128
+    bf16, f32 = jnp.bfloat16, jnp.float32
+    row = places * tokens
+    each = width // (2 * count)
+    anywhere, vmem = pl.BlockSpec(memory_space=pl.ANY), pl.BlockSpec(memory_space=pltpu.VMEM)
+    shape = jax.ShapeDtypeStruct
+    chunks = (2 * count, tokens, each)
+    return pl.pallas_call(
+        functools.partial(attend_kernel, chain, places),
+        out_shape=[
+            shape((gate_weight.shape[0] * 8, gate_weight.shape[1]), bf16),
+            shape((up_weight.shape[0] * 8, up_weight.shape[1]), bf16),
+            shape((down_weight.shape[0], down_weight.shape[1] * 8), bf16),
+            shape((in_weight.shape[0] * 8, wide), bf16),
+            shape((out_weight.shape[0], out_weight.shape[1] * 8), bf16),
+            shape(chunks, bf16),
+            shape((tokens, width), bf16),
+            shape((tokens, heads_wide), bf16),
+            shape((row, 128), bf16),
+            shape((tokens, heads_wide), f32),
+            shape((tokens, 128), f32),
+            shape((tokens, 128), f32),
+            shape((tokens, 128), f32),
+            shape((8,) + small.shape, f32),
+        ],
+        in_specs=[vmem, vmem] + [anywhere] * 5 + [vmem],
+        out_specs=[anywhere] * 5 + [vmem] * 8 + [vmem],
+        scratch_shapes=[
+            pltpu.VMEM((in_weight.shape[0] * 8, wide), bf16),
+            pltpu.VMEM((out_weight.shape[0], out_weight.shape[1] * 8), bf16),
+            pltpu.VMEM((8, width), f32),
+            pltpu.VMEM((2, row, 128), bf16),
+            pltpu.VMEM((2, row, 128), bf16),
+            pltpu.VMEM((row, 128), f32),
+            pltpu.VMEM((places, tokens, tokens), f32),
+            pltpu.VMEM((tokens, 128), f32),
+            pltpu.VMEM((tokens, 128), f32),
+            pltpu.VMEM((places, tokens, 128), bf16),
+            pltpu.VMEM(chunks, bf16),
+            pltpu.VMEM(chunks, bf16),
+            pltpu.VMEM(chunks, bf16),
+            pltpu.SemaphoreType.DMA((2, 7)),
+            pltpu.SemaphoreType.DMA((2, 5, Gather.COPIES)),
+            pltpu.SemaphoreType.DMA((7,)),
+            pltpu.SemaphoreType.DMA((2, places)),
+            pltpu.SemaphoreType.DMA((2, 4, count)),
+        ],
+        compiler_params=pltpu.CompilerParams(
+            collective_id=0, has_side_effects=True, vmem_limit_bytes=VMEM_BYTES
+        ),
+        name="attend_forward",
+    )(x, small, in_weight, out_weight, gate_weight, up_weight, down_weight, inverse)
 
 
 class Scatter:
@@ -726,57 +1022,66 @@
 ):
     row_count = inputs.shape[0]
     head_size = key_weight.shape[1]
-    heads_here = query_weight.shape[1] // head_size
-    myself = lax.axis_index("tokens")
+    query_width = query_weight.shape[1]
+    heads_here = query_width // head_size
+    places = ROW // row_count
     small = jnp.stack(
         [
             segments.astype(jnp.float32),
             jnp.concatenate([pre_gain, mid_gain]).astype(jnp.float32),
         ]
     )
-    small = jnp.concatenate([small, jnp.zeros((14, row_count), jnp.float32)])
+    small = jnp.concatenate([small, jnp.zeros((6, row_count), jnp.float32)])
     in_weight = jnp.concatenate([query_weight, key_weight, value_weight], axis=1)
-    small_full, in_full, out_full, gate_full, up_full, down_full = gather_weights(
-        (small, in_weight, out_weight, gate_weight, up_weight, down_weight), (0, 0, 1, 0, 0, 1), 0
-    )
-    query_width = query_weight.shape[1]
+    half_size = head_size // 2
+    inverse = 10000.0 ** (-jnp.arange(half_size, dtype=jnp.float32) / half_size)
+    inverse = jnp.broadcast_to(jnp.tile(inverse, 128 // half_size)[None], (8, 128))
+    (
+        gate_full,
+        up_full,
+        down_full,
+        in_full,
+        out_full,
+        attn_sum,
+        normed,
+        query_rot,
+        pairs,
+        attended,
+        log_total,
+        cos_wide,
+        sin_wide,
+        small_full,
+    ) = attend(
+        chain, places, inputs, small, in_weight, out_weight, gate_weight, up_weight, down_weight, inverse
+    )
     query_full = in_full[:, :query_width]
     key_full = in_full[:, query_width : query_width + head_size]
     value_full = in_full[:, query_width + head_size :]
-    small_full = small_full.reshape(8, 16, row_count)
     all_ids = small_full[:, 0].reshape(-1).astype(jnp.int32)
     pre_row = small_full[:, 1, : row_count // 2].reshape(-1)
     mid_row = small_full[:, 1, row_count // 2 :].reshape(-1)
+    myself = lax.axis_index("tokens")
+    own_first = myself * row_count
+    own_places = own_first + jnp.arange(row_count, dtype=jnp.int32)
+    row_start = own_first // ROW * ROW
     length = all_ids.shape[0]
-    places = jnp.arange(length, dtype=jnp.int32)
-    starts_here = jnp.concatenate([jnp.ones((1,), dtype=jnp.bool_), all_ids[1:] != all_ids[:-1]])
-    opening = lax.cummax(jnp.where(starts_here, places, 0), axis=0)
-    own_first = myself * row_count
-    positions = lax.dynamic_slice_in_dim(places - opening, own_first, row_count)
-    own_places = own_first + jnp.arange(row_count, dtype=jnp.int32)
-    half_size = head_size // 2
-    inverse = 10000.0 ** (-jnp.arange(half_size, dtype=jnp.float32) / half_size)
-    turned = positions.astype(jnp.float32)[:, None] * inverse[None, :]
-    cos_table = jnp.cos(turned)[:, None, :]
-    sin_table = jnp.sin(turned)[:, None, :]
+    span = math.gcd(ROW, 1024)
+    block_first = row_start // span
+    block_total = (own_first + row_count + span - 1) // span
+    key_all = lax.dynamic_update_slice_in_dim(
+        jnp.zeros((length, head_size), jnp.bfloat16), pairs[:, :head_size], row_start, 0
+    )
+    value_all = lax.dynamic_update_slice_in_dim(
+        jnp.zeros((length, head_size), jnp.bfloat16), pairs[:, head_size:], row_start, 0
+    )
+    cos_table = cos_wide[:, None, :half_size]
+    sin_table = sin_wide[:, None, half_size : 2 * half_size]
     inputs_f = inputs.astype(jnp.float32)
     pre_scale = rms_scale(inputs_f)
-    normed = (inputs_f * pre_scale * pre_row).astype(jnp.bfloat16)
-    queries = jnp.dot(normed, query_full, preferred_element_type=jnp.float32).reshape(
-        row_count, heads_here, head_size
-    )
-    query_rot = (rotate(queries, cos_table, sin_table) * head_size ** (-0.5)).astype(jnp.bfloat16)
-    key_rows = jnp.dot(normed, key_full, preferred_element_type=jnp.float32)[:, None, :]
-    key_rot = rotate(key_rows, cos_table, sin_table)[:, 0, :].astype(jnp.bfloat16)
-    value_low = jnp.dot(normed, value_full, preferred_element_type=jnp.float32).astype(jnp.bfloat16)
-    key_all, value_all = (
-        lax.all_gather(key_rot, "tokens", axis=0, tiled=True),
-        lax.all_gather(value_low, "tokens", axis=0, tiled=True),
-    )
-    span = math.gcd(ROW, 1024)
-    row_start = own_first // ROW * ROW
-    block_first = row_start // span
-    block_total = (own_first + row_count + span - 1) // span
+    attended_low = attended.astype(jnp.bfloat16)
+    attended = attended.reshape(row_count, heads_here, head_size)
+    query_rot = query_rot.reshape(row_count, heads_here, head_size)
+    log_total = log_total[:, :heads_here]
 
     def key_block(block_index):
         opening_row = block_index * span
@@ -792,34 +1097,8 @@
         )
         return (opening_row, block_keys, block_values, allowed[:, None, :], scores)
 
-    def forward_step(block_index, state_now):
-        row_peak, row_total, running = state_now
-        opening_row, block_keys, block_values, allowed, scores = key_block(block_index)
-        new_peak = jnp.maximum(row_peak, jnp.max(jnp.where(allowed, scores, -1e30), axis=-1))
-        factor = jnp.exp(row_peak - new_peak)
-        weights = jnp.where(allowed, jnp.exp(scores - new_peak[..., None]), 0.0)
-        row_total = row_total * factor + jnp.sum(weights, axis=-1)
-        running = running * factor[..., None] + jnp.einsum(
-            "qhk,kd->qhd",
-            weights.astype(jnp.bfloat16),
-            block_values,
-            preferred_element_type=jnp.float32,
-        )
-        return (new_peak, row_total, running)
-
-    start_state = (
-        jnp.full((row_count, heads_here), -1e30, jnp.float32),
-        jnp.zeros((row_count, heads_here), jnp.float32),
-        jnp.zeros((row_count, heads_here, head_size), jnp.float32),
-    )
-    row_peak, row_total, running = lax.fori_loop(
-        block_first, block_total, forward_step, start_state
-    )
-    attended = running / row_total[..., None]
-    log_total = row_peak + jnp.log(row_total)
-    attended_low = attended.astype(jnp.bfloat16).reshape(row_count, heads_here * head_size)
-    attn_term = jnp.dot(attended_low, out_full, preferred_element_type=jnp.float32)
-    middle = inputs_f + chain_sum(attn_term.astype(jnp.bfloat16), chain, 1).astype(jnp.float32)
+    attn_term = attn_sum.transpose(1, 0, 2).reshape(row_count, -1)
+    middle = inputs_f + attn_term.astype(jnp.float32)
     mid_scale = rms_scale(middle)
     normed_mid = (middle * mid_scale * mid_row).astype(jnp.bfloat16)
     gate_rows = jnp.dot(normed_mid, gate_full, preferred_element_type=jnp.float32)

time: 1550 us -> 717 us (0.46)
  Pallas kernels: 1300 us -> 429 us
  local copies, waits for them, and re-layouts: 17.1 us -> 58.5 us
  waiting for transfers between devices: 0.02 us -> 30.3 us
  blocking collectives: 32.8 us -> 12.1 us
  matrix products: 123 us -> 107 us
    pallas_call x5 -> x4, Pallas kernels: 1150 us -> 331 us  [the longest x3 202 us: chain_sum(): pl.pallas_call(functools.partial(chain_kernel, chain, count), out_shape=j...]
    pallas_call x1, Pallas kernels: 150 us -> 97.5 us  [scatter_sums(): pl.pallas_call(functools.partial(scatter_kernel, axes), out_shape=[jax.Sh...]
    reduce_scatter x1, waiting for transfers between devices: 0.01 us -> 30.3 us  [shards_cube(): lax.psum_scatter(back_pairs.astype(jnp.bfloat16), 'tokens', scatter_dimen...]
    convert_element_type x0 -> x4, local copies, waits for them, and re-layouts: none -> 22.3 us  [the longest x1 5.87 us: shards_cube(): middle = inputs_f + attn_term.astype(jnp.float32)]
    all_gather x2 -> x0, blocking collectives: 20.8 us -> none  [the longest x1 10.4 us: shards_cube(): lax.all_gather(key_rot, 'tokens', axis=0, tiled=True)]
    dot_general x5 -> x0, matrix products: 18.6 us -> none  [the longest x1 9.93 us: forward_step(): jnp.einsum('qhk,kd->qhd', weights.astype(jnp.bfloat16), block_values, pre...]
  transfers between devices with their start and end apart: 1 -> 1, of which waited for: 0 -> 1; matrix products, arithmetic and copies ran while one was open for 2% -> 5% of each run, Pallas kernels for 16% -> 0%
where the time goes in v2:
time: 717 us; the launch traced here: 707 us
  Pallas kernels  429 us (60%)
  matrix products  107 us (15%)
  local copies, waits for them, and re-layouts  58.5 us (8%)
  other arithmetic  54.1 us (8%)
  waiting for transfers between devices  30.3 us (4%)
  between operations  15.5 us (2%)
  blocking collectives  12.1 us (2%)
    pallas_call x3, Pallas kernels, chain_sum(): pl.pallas_call(functools.partial(chain_kernel, chain, count), out_shape=j...  202 us
    pallas_call x1, Pallas kernels, attend(): pl.pallas_call(functools.partial(attend_kernel, chain, places), out_shape...  130 us
    pallas_call x1, Pallas kernels, scatter_sums(): pl.pallas_call(functools.partial(scatter_kernel, axes), out_shape=[jax.Sh...  97.5 us
    reduce_scatter x1, waiting for transfers between devices, shards_cube(): lax.psum_scatter(back_pairs.astype(jnp.bfloat16), 'tokens', scatter_dimen...  30.3 us
    unnamed x96, local copies, waits for them, and re-layouts  21 us
  transfers between devices with their start and end apart: 1, of which 1 were waited for; matrix products, arithmetic and copies ran while one was open for 5% of the time, Pallas kernels for 0%

profile of v2, /device:TPU:0, one launch (start us, length us, event | category | flops | bytes accessed | tf_op | source)
XLA Modules:
  0.0 707.1 jit_solution(11359287308037283647)
XLA Ops:
  11.1 2.9 copy.103
  16.4 129.6 %attend_forward.1 = (bf16[2048,1408]{1,0:T(8,128)(2,1)}, bf16[2048,1408]{1,0:T(8,128)(2,1)}, bf16[1408,2048]{1,0:T(8,128)(2,1)}, bf16[2048,640]{1,0:T(8,128)(2,1...) custom-call(bf16[512,2048]{1,0:T(8,128)(2,1)} %x.1, ...), custom_call_target="tpu_custom_call" | custom-call | tf_op jit(solution)/shard_map/attend_forward/pallas_call | solution.py:830
  148.4 4.0 convert_bitcast_fusion
  152.4 5.9 copy.106
  158.3 3.2 multiply_reduce_fusion.2
  162.6 9.5 %fusion.54 = f32[512,1408]{1,0:T(8,128)} fusion(bf16[512,2048]{0,1:T(8,128)(2,1)S(1)} %multiply_convert_fusion, bf16[2048,1408]{1,0:T(8,128)(2,1)} %get-tuple-element.102), kind=kOutput, calls=%fused_computation.113 | convolution fusion | flops 2952790016 | bytes 10747904 | tf_op jit(solution)/shard_map/dot_general | solution.py:1105
  172.2 5.1 fusion.53
  177.3 2.5 copy.110
  179.8 8.9 %multiply_convert_fusion.1 = (bf16[512,1408]{1,0:T(8,128)(2,1)S(1)}, bf16[512,1408]{1,0:T(8,128)(2,1)S(1)}, bf16[512,1408]{1,0:T(8,128)(2,1)}) fusion(f32[512,1408]{1,0:T(8,128)} %fusion.53, f32[512,1408]{1,0:T(8,128)} %fusion.54, bf16[1408,2048]{1,0:T(8,128)(2,1)} %get-tuple-element.103, bf16[512,2048]{1,0:T(8,128)(2,1)S(1)} %copy-done.13), kind=kOutput, calls=%fused_computation.56 | convolution fusion | flops 2963603456 | bytes 17956864 | tf_op jit(solution)/shard_map/td,fd->tf/dot_general | solution.py:1114
  188.8 6.5 fusion.55
  195.3 7.3 %add_convert_fusion.1 = bf16[512,2048]{1,0:T(8,128)(2,1)} fusion(f32[512,2048]{1,0:T(8,128)S(1)} %fusion.55, bf16[512,1408]{1,0:T(8,128)(2,1)S(1)} %get-tuple-element.280, bf16[2048,1408]{1,0:T(8,128)(2,1)} %get-tuple-element.102), kind=kOutput, calls=%fused_computation.48 | convolution fusion | flops 2954887168 | bytes 13500416 | tf_op jit(solution)/shard_map/tf,cf->tc/dot_general | solution.py:1123
  202.6 68.2 %chain_sum.4 = bf16[16,32,2048]{2,1,0:T(8,128)(2,1)} custom-call(bf16[16,32,2048]{2,1,0:T(8,128)(2,1)} %bitcast.146), custom_call_target="tpu_custom_call" | custom-call | tf_op jit(solution)/shard_map/chain_sum/pallas_call | solution.py:530
  270.9 4.2 bitcast_convert_fusion.1
  275.0 5.4 copy.109
  280.5 4.8 multiply_reduce_fusion
  285.6 4.6 convolution_convert_fusion.5
  290.1 64.6 %chain_sum.3 = bf16[16,32,2048]{2,1,0:T(8,128)(2,1)} custom-call(bf16[16,32,2048]{2,1,0:T(8,128)(2,1)} %bitcast.147), custom_call_target="tpu_custom_call" | custom-call | tf_op jit(solution)/shard_map/chain_sum/pallas_call | solution.py:530
  354.8 4.2 bitcast_convert_fusion
  358.9 5.5 copy.107
  367.8 7.4 %convert_add_fusion.1 = (f32[512,2048]{0,1:T(8,128)S(1)}, bf16[512,2048]{0,1:T(8,128)(2,1)}) fusion(bf16[512,2048]{0,1:T(8,128)(2,1)} %copy.110, f32[512,2048]{0,1:T(8,128)} %copy.109, f32[512,2048]{0,1:T(8,128)} %copy-done, f32[512]{0:T(512)S(1)} %broadcast_multiply_fusion.1, f32[2048]{0:T(1024)S(1)} %bitcast.152, f32[512]{0:T(512)S(1)} %get-tuple-element.299, ...), kind=kLoop, calls=%fused_computation.46 | loop fusion | flops 9437184 | bytes 20983808 | tf_op jit(solution)/shard_map/add | solution.py:1126
  375.2 2.2 multiply_reduce_fusion.3
  378.9 28.0 %while.13 = (s32[]{:T(128)}, f32[512,8,64]{0,2,1:T(8,128)S(1)}, f32[4096,128]{1,0:T(8,128)}, s32[]{:T(128)}, s32[512]{0:T(512)S(1)}, /*index=5*/s32[4096]{0:T(10...) while((s32[]{:T(128)}, f32[512,8,64]{0,2,1:T(8,128)S(1)}, ...), condition=%wide.region_5.6_spmd.clone, body=%wide.region_4.5_spmd.clone.sunk | while | flops 2720007680 | bytes 94316856 | solution.py:1165
  379.9 2.4 fusion.109
  382.2 7.6 %fusion.110 = bf16[512,8,1024]{0,2,1:T(8,128)(2,1)} fusion(f32[1024,512,8]{1,0,2:T(8,128)S(1)} %fusion.109, bf16[512,8,64]{0,2,1:T(8,128)(2,1)S(1)} %copy-done.32, f32[512,8]{0,1:T(8,128)S(1)} %get-tuple-element.425, f32[512,8]{0,1:T(8,128)S(1)} %get-tuple-element.422, pred[512,1024]{0,1:T(8,128)(4,1)S(1)} %compare_and_fusion.2, ...), kind=kOutput, calls=%fused_computation.2.clone.1 | convolution fusion | flops 557842432 | bytes 26378244 | tf_op jit(solution)/shard_map/while/body/qhd,kd->qhk/dot_general | solution.py:1146
  389.9 6.0 convolution_bitcast_fusion.3
  395.9 3.0 fusion.111
  401.3 5.2 convolution_add_fusion.2
  406.9 2.7 convert_element_type.163
  409.7 4.9 convolution_convert_fusion.3.refs_4_
  414.7 5.2 convolution_convert_fusion.1.refs_1_
  421.9 2.4 copy.125
  424.6 5.1 fusion.32
  430.9 2.6 convolution_convert_fusion.4
  433.6 5.2 convolution_convert_fusion.2.refs_0_
  438.7 5.2 convolution_convert_fusion.refs_2_
  443.9 30.3 %reduce-scatter.2.cloned.1.call-done = bf16[512,128]{1,0:T(8,128)(2,1)} async-done(((bf16[4096,128]{1,0:T(8,128)(2,1)}), bf16[512,128]{1,0:T(8,128)(2,1)}) %reduce-scatter.2.cloned.1.call-update) | async-done | bytes 131088 | tf_op jit(solution)/shard_map/reduce_scatter | solution.py:1166
  477.2 3.5 pad_maximum_fusion.refs_3_
  480.6 97.5 %scatter_sums.1 = (f32[256,1408]{1,0:T(8,128)}, f32[256,1408]{1,0:T(8,128)}, f32[1408,256]{1,0:T(8,128)}, f32[256,640]{1,0:T(8,128)}, f32[512,256]{1,0:T(8,128)}) custom-call(bf16[2048,1408]{1,0:T(8,128)(2,1)} %convolution_convert_fusion.2.refs_0_, bf16[2048,1408]{1,0:T(8,128)(2,1)} %convolution_convert_fusion.1.refs_1_, ...), custom_call_target="tpu_custom_call" | custom-call | tf_op jit(solution)/shard_map/scatter_sums/pallas_call | solution.py:989
  578.1 1.9 slice.79
  581.0 3.8 fusion.39
  586.2 5.7 add_convert_fusion
  592.0 68.8 %chain_sum.5 = bf16[16,32,2048]{2,1,0:T(8,128)(2,1)} custom-call(bf16[16,32,2048]{2,1,0:T(8,128)(2,1)} %bitcast.143), custom_call_target="tpu_custom_call" | custom-call | tf_op jit(solution)/shard_map/chain_sum/pallas_call | solution.py:530
  660.8 4.1 bitcast_convert_fusion.2
  665.0 5.5 copy.119
  670.5 2.9 fusion.29
  673.5 12.1 %all-reduce.2 = (bf16[2048]{0:T(1024)(128)(2,1)S(1)}, bf16[2048]{0:T(1024)(128)(2,1)S(1)}) all-reduce(bf16[2048]{0:T(1024)(128)(2,1)S(1)} %get-tuple-element.248, bf16[2048]{0:T(1024)(128)(2,1)S(1)} %copy-done.30), channel_id=3, replica_groups=mesh['tokens'=8,'heads'=4] {'tokens'}, use_global_device_ids=true, to_apply=%region_9.10.clone | all-reduce | flops 4096 | bytes 16384
  686.8 5.0 fusion.28
  691.9 4.1 copy.126
  (154 shorter events, 31.8 us)
Async XLA Ops:
  7.2 6.9 copy-start.26
  7.2 467.0 %reduce-scatter.2.cloned.1.call-start = ((), (), s32[]{:S(2)}) async-start(), calls=%async_computation.1 | async-start | bytes 1179648 | tf_op jit(solution)/shard_map/reduce_scatter | solution.py:1166
  14.0 144.3 %copy-start.2 = (bf16[512,2048]{0,1:T(8,128)(2,1)}, bf16[512,2048]{0,1:T(8,128)(2,1)S(1)}, u32[]{:S(2)}) copy-start(bf16[512,2048]{0,1:T(8,128)(2,1)S(1)} %copy.103) | copy-start | bytes 6291460
  161.5 10.7 %copy-start = (f32[512,2048]{0,1:T(8,128)}, f32[512,2048]{0,1:T(8,128)S(1)}, u32[]{:S(2)}) copy-start(f32[512,2048]{0,1:T(8,128)S(1)} %get-tuple-element.279) | copy-start | bytes 12582916
  162.1 10.0 %slice-start.2 = ((s8[5767168]{0:T(1024)(128)(4,1)}), s8[4194304]{0:T(1024)(128)(4,1)S(1)}, s32[]{:S(2)}) async-start(s8[5767168]{0:T(1024)(128)(4,1)} %bitcast.159), calls=%async_computation.4 | async-start | bytes 8388608
  162.6 9.6 %copy-start.10 = (bf16[512,2048]{0,1:T(8,128)(2,1)}, bf16[512,2048]{0,1:T(8,128)(2,1)S(1)}, u32[]{:S(2)}) copy-start(bf16[512,2048]{0,1:T(8,128)(2,1)S(1)} %multiply_convert_fusion) | copy-start | bytes 6291460
  162.6 9.6 %slice-start.3 = ((s8[5767168]{0:T(1024)(128)(4,1)}), s8[1572864]{0:T(1024)(128)(4,1)S(1)}, s32[]{:S(2)}) async-start(s8[5767168]{0:T(1024)(128)(4,1)} %bitcast.159), calls=%async_computation.5 | async-start | bytes 3145728
  172.2 5.1 copy-start.13
  188.8 6.5 copy-start.36
  188.8 6.6 copy-start.38
  275.0 10.3 %slice-start = ((s8[5767168]{0:T(1024)(128)(4,1)}), s8[1572864]{0:T(1024)(128)(4,1)S(1)}, s32[]{:S(2)}) async-start(s8[5767168]{0:T(1024)(128)(4,1)} %bitcast.157), calls=%async_computation.2 | async-start | bytes 3145728
  280.5 4.8 slice-start.1
  280.5 5.1 copy-start.34
  358.9 5.5 copy-start.8
  358.9 5.9 copy-start.15
  364.4 2.3 copy-start.25
  366.9 0.8 copy-start.23
  367.8 7.4 %copy-start.31 = (bf16[512,2048]{1,0:T(8,128)(2,1)S(1)}, bf16[512,2048]{1,0:T(8,128)(2,1)}, u32[]{:S(2)}) copy-start(bf16[512,2048]{1,0:T(8,128)(2,1)} %get-tuple-element.107) | copy-start | bytes 6291460
  375.1 2.2 copy-start.1
  375.2 3.7 copy-start.27
  378.9 3.3 copy-start.6
  379.8 2.4 copy-start.32
  401.3 5.2 copy-start.7
  406.9 2.8 copy-start.9
  409.7 5.0 copy-start.11
  409.7 5.0 copy-start.39
  414.6 5.2 copy-start.21
  414.6 7.1 %copy-start.20 = (f32[512,128]{1,0:T(8,128)S(1)}, f32[512,128]{1,0:T(8,128)}, u32[]{:S(2)}) copy-start(f32[512,128]{1,0:T(8,128)} %get-tuple-element.110) | copy-start | bytes 786436
  414.6 7.2 %copy-start.5 = (bf16[512,2048]{0,1:T(8,128)(2,1)S(1)}, bf16[512,2048]{0,1:T(8,128)(2,1)}, u32[]{:S(2)}) copy-start(bf16[512,2048]{0,1:T(8,128)(2,1)} %get-tuple-element.284) | copy-start | bytes 6291460
  424.5 5.1 copy-start.33
  424.6 6.3 copy-start.4
  430.9 2.7 copy-start.12
  430.9 2.6 copy-start.37
  433.5 5.2 copy-start.14
  433.6 5.2 copy-start.35
  438.7 36.4 %copy-start.22 = (f32[512,128]{1,0:T(8,128)S(1)}, f32[512,128]{1,0:T(8,128)}, u32[]{:S(2)}) copy-start(f32[512,128]{1,0:T(8,128)} %get-tuple-element.111) | copy-start | bytes 786436
  474.2 2.1 copy-start.19
  665.0 5.5 copy-start.3
  665.0 5.5 copy-start.28
  665.0 5.5 copy-start.29
  670.5 3.0 copy-start.30
  691.8 4.1 copy-start.24
  691.9 4.9 copy-start.18
  691.9 6.0 copy-start.17
  695.9 3.0 copy-start.16
Sparse Core Ops, SparseCore 0:
  409.8 64.3 reduce-scatter.1

commit v3 on v2

--- a/solution.py
+++ b/solution.py
@@ -303,7 +303,7 @@
 
 
 MESH_ID = pl.DeviceIdType.MESH
-VMEM_BYTES = 60 * 2**20
+VMEM_BYTES = 63 * 2**20
 
 
 def token_device(flip):
@@ -314,13 +314,6 @@
     return pltpu.make_async_remote_copy(
         src_ref=src, dst_ref=dst, send_sem=send, recv_sem=recv, device_id=device, device_id_type=MESH_ID
     )
-
-
-def greet_cube():
-    barrier = pltpu.get_barrier_semaphore()
-    for flip in (1, 2, 4):
-        pl.semaphore_signal(barrier, inc=1, device_id=token_device(flip), device_id_type=MESH_ID)
-    pl.semaphore_wait(barrier, 3)
 
 
 def block_of(ref, axis, index, half=None):
@@ -403,32 +396,6 @@
         self.own_copy().wait()
 
 
-def greet_chain(chain):
-    here = lax.axis_index("heads")
-    barrier = pltpu.get_barrier_semaphore()
-    for step in (-1, 1):
-        near = here + step
-
-        @pl.when((near >= 0) & (near < chain))
-        def _():
-            pl.semaphore_signal(
-                barrier,
-                inc=1,
-                device_id=(lax.axis_index("tokens"), near),
-                device_id_type=MESH_ID,
-            )
-
-    edge = (here == 0) | (here == chain - 1)
-
-    @pl.when(edge)
-    def _():
-        pl.semaphore_wait(barrier, 1)
-
-    @pl.when(jnp.logical_not(edge))
-    def _():
-        pl.semaphore_wait(barrier, 2)
-
-
 class ChainSum:
     def __init__(self, chain, upward, term, passing, total, base, count, sems):
         self.chain, self.term, self.passing, self.total = chain, term, passing, total
@@ -506,42 +473,6 @@
         def _():
             for i in range(self.count):
                 self.back_copy(i).wait_send()
-
-
-def chain_kernel(chain, count, term, out, passing, total, sems):
-    greet_chain(chain)
-    sums = [
-        ChainSum(chain, upward, term, passing, total, base, count, sems.at[k])
-        for k, (upward, base) in enumerate(((True, 0), (False, count)))
-    ]
-
-    @pl.loop(0, sums[0].steps())
-    def _(now):
-        for part in sums:
-            part.step(now)
-
-    for part in sums:
-        part.finish()
-    out[...] = total[...]
-
-
-def chain_sum(term, chain, collective_id, count=8):
-    shape = (2 * count, term.shape[0] // (2 * count), term.shape[1])
-    return pl.pallas_call(
-        functools.partial(chain_kernel, chain, count),
-        out_shape=jax.ShapeDtypeStruct(shape, term.dtype),
-        in_specs=[pl.BlockSpec(memory_space=pltpu.VMEM)],
-        out_specs=pl.BlockSpec(memory_space=pltpu.VMEM),
-        scratch_shapes=[
-            pltpu.VMEM(shape, term.dtype),
-            pltpu.VMEM(shape, term.dtype),
-            pltpu.SemaphoreType.DMA((2, 4, count)),
-        ],
-        compiler_params=pltpu.CompilerParams(
-            collective_id=collective_id, has_side_effects=True, vmem_limit_bytes=VMEM_BYTES
-        ),
-        name="chain_sum",
-    )(term.reshape(shape)).reshape(term.shape)
 
 
 def lanes(shape):
@@ -874,58 +805,53 @@
     )(x, small, in_weight, out_weight, gate_weight, up_weight, down_weight, inverse)
 
 
-class Scatter:
-    COPIES = 10
-
-    def __init__(self, grad, axis, own, sib, near, sems, local):
-        self.grad, self.axis, self.own, self.sib, self.near = grad, axis, own, sib, near
-        self.sems, self.local = sems, local
-        self.me = lax.axis_index("tokens")
-
-    def sib_copy(self, k):
-        index = jnp.bitwise_xor(self.me, 2 * k + 1)
+def greet(flips, chain):
+    me, here = lax.axis_index("tokens"), lax.axis_index("heads")
+    barrier = pltpu.get_barrier_semaphore()
+    for flip in flips:
+        pl.semaphore_signal(barrier, inc=1, device_id=token_device(flip), device_id_type=MESH_ID)
+    for step in (-1, 1):
+        near = here + step
+
+        @pl.when((near >= 0) & (near < chain))
+        def _():
+            pl.semaphore_signal(barrier, inc=1, device_id=(me, near), device_id_type=MESH_ID)
+
+    edge = (here == 0) | (here == chain - 1)
+
+    @pl.when(edge)
+    def _():
+        pl.semaphore_wait(barrier, len(flips) + 1)
+
+    @pl.when(jnp.logical_not(edge))
+    def _():
+        pl.semaphore_wait(barrier, len(flips) + 2)
+
+
+class Reduce:
+    COPIES = 6
+
+    def __init__(self, own, near, sems):
+        self.own, self.near, self.sems = own, near, sems
+
+    def copy(self, slot):
+        k, half, flip = ((1, 0, 2), (3, 0, 2), (2, 1, 4), (3, 1, 4), (2, 0, 4), (1, 1, 2))[slot]
+        rows = self.own.shape[1] // 2
         return remote(
-            block_of(self.grad, self.axis, index),
-            self.sib.at[k],
-            self.sems.at[0, k],
-            self.sems.at[1, k],
-            token_device(1),
-        )
-
-    def own_copy(self, k):
-        index = jnp.bitwise_xor(self.me, 2 * k)
-        return pltpu.make_async_copy(
-            block_of(self.grad, self.axis, index), self.own.at[k], self.local.at[k]
-        )
-
-    def half(self, ref, k, half):
-        rows = ref.shape[1] // 2
-        return ref.at[k, pl.ds(half * rows, rows)]
-
-    def chip_copy(self, slot):
-        k, half, flip = ((1, 0, 2), (3, 0, 2), (2, 1, 4), (3, 1, 4), (2, 0, 4), (1, 1, 2))[slot]
-        return remote(
-            self.half(self.own, k, half),
+            self.own.at[k, pl.ds(half * rows, rows)],
             self.near.at[slot],
-            self.sems.at[0, 4 + slot],
-            self.sems.at[1, 4 + slot],
+            self.sems.at[0, slot],
+            self.sems.at[1, slot],
             token_device(flip),
         )
 
-    def start(self):
-        for k in (3, 1, 2, 0):
-            self.sib_copy(k).start()
-            self.own_copy(k).start()
-
-    def cores(self):
-        for k in (3, 1, 2, 0):
-            self.sib_copy(k).wait_recv()
-            self.own_copy(k).wait()
-            self.own[k] = (
-                self.own[k].astype(jnp.float32) + self.sib[k].astype(jnp.float32)
-            ).astype(self.own.dtype)
-            for slot in {3: (1, 3), 1: (0,), 2: (2,), 0: ()}[k]:
-                self.chip_copy(slot).start()
+    def put(self, k, block):
+        self.own[k] = block.astype(self.own.dtype)
+        self.send(k)
+
+    def send(self, k):
+        for slot in {3: (1, 3), 1: (0,), 2: (2,), 0: ()}[k]:
+            self.copy(slot).start()
 
     def add_near(self, k, half, slot):
         rows = self.own.shape[1] // 2
@@ -935,12 +861,12 @@
         ).astype(self.own.dtype)
 
     def second(self):
-        self.chip_copy(1).wait_recv()
+        self.copy(1).wait_recv()
         self.add_near(2, 0, 1)
-        self.chip_copy(4).start()
-        self.chip_copy(3).wait_recv()
+        self.copy(4).start()
+        self.copy(3).wait_recv()
         self.add_near(1, 1, 3)
-        self.chip_copy(5).start()
+        self.copy(5).start()
 
     def finish(self, out):
         rows = self.own.shape[1] // 2
@@ -948,61 +874,679 @@
             place = pl.ds(half * rows, rows)
             total = self.own[0, place].astype(jnp.float32)
             for slot in slots:
-                self.chip_copy(slot).wait_recv()
+                self.copy(slot).wait_recv()
                 total = total + self.near[slot].astype(jnp.float32)
             out[place, :] = total
-        for k in range(4):
-            self.sib_copy(k).wait_send()
-        for slot in range(6):
-            self.chip_copy(slot).wait_send()
-
-
-def scatter_kernel(axes, *refs):
-    count = len(axes)
-    grads, outs = refs[:count], refs[count : 2 * count]
-    owns = refs[2 * count : 3 * count]
-    sibs = refs[3 * count : 4 * count]
-    nears = refs[4 * count : 5 * count]
-    sems, local = refs[5 * count :]
-    greet_cube()
-    parts = [
-        Scatter(grads[i], axes[i], owns[i], sibs[i], nears[i], sems.at[i], local.at[i])
-        for i in range(count)
+        for slot in range(self.COPIES):
+            self.copy(slot).wait_send()
+
+
+def tn_dot(left, right):
+    return lax.dot_general(
+        left, right, (((0,), (0,)), ((), ())), preferred_element_type=jnp.float32
+    )
+
+
+def tiles_of(length, size):
+    return [(low, min(low + size, length)) for low in range(0, length, size)]
+
+
+def feed_kernel(
+    chain, x, attn_sum, small_all, cotangent, gate_full, up_full, down_full, back_attn, hidden, mlp_term,
+    grad_gate, grad_up, grad_mid, gate, up, down, mid_row, normed, back_gate, back_up, term, passing, total,
+    own_gate, near_gate, own_up, near_up, load_sems, swap_sems, chain_sems, reduce_sems,
+):
+    count = term.shape[0] // 2
+    each = term.shape[2]
+    tokens, width = x.shape
+    inner = gate.shape[1]
+    me = lax.axis_index("tokens")
+    tiles = tiles_of(inner, 512)
+    loads = []
+    for k, (low, high) in enumerate(tiles):
+        cut = pl.ds(low, high - low)
+        loads.append(
+            (
+                pltpu.make_async_copy(gate_full.at[:, cut], gate.at[:, cut], load_sems.at[0, k]),
+                pltpu.make_async_copy(up_full.at[:, cut], up.at[:, cut], load_sems.at[1, k]),
+                pltpu.make_async_copy(down_full.at[cut, :], down.at[cut, :], load_sems.at[2, k]),
+            )
+        )
+    for group in loads:
+        for load in group:
+            load.start()
+    greet((1, 2, 4), chain)
+
+    def swap(k, ref, cut):
+        mine, theirs = pl.ds(0, tokens), pl.ds(tokens, tokens)
+        return remote(
+            ref.at[mine, cut],
+            ref.at[theirs, cut],
+            swap_sems.at[0, k],
+            swap_sems.at[1, k],
+            token_device(1),
+        )
+
+    span = width // 8
+    for k in range(8):
+        mid_row[:, k * span : (k + 1) * span] = jnp.broadcast_to(
+            small_all[k, 1:2, span : 2 * span], (8, span)
+        )
+
+    def middle_at(c):
+        cut = slice(c * each, (c + 1) * each)
+        return x[:, cut].astype(jnp.float32) + attn_sum[c].astype(jnp.float32)
+
+    squares = jnp.zeros((tokens, each), jnp.float32)
+    for c in range(2 * count):
+        part = middle_at(c)
+        squares = squares + part * part
+    mid_scale = lax.rsqrt(jnp.sum(squares, axis=1, keepdims=True) / width + 1e-05)
+    for c in range(2 * count):
+        cut = slice(c * each, (c + 1) * each)
+        normed[:tokens, cut] = (middle_at(c) * mid_scale * mid_row[0:1, cut]).astype(jnp.bfloat16)
+    swaps = [swap(0, normed, pl.ds(0, width))]
+    swaps[0].start()
+
+    for k, (low, high) in enumerate(tiles):
+        for load in loads[k]:
+            load.wait()
+        gate_rows = jnp.dot(
+            normed[:tokens, :], gate[:, low:high], preferred_element_type=jnp.float32
+        )
+        up_rows = jnp.dot(normed[:tokens, :], up[:, low:high], preferred_element_type=jnp.float32)
+        back_hidden = nt_dot(cotangent[...], down[low:high, :])
+        sigmoid = jax.nn.sigmoid(gate_rows)
+        silu = gate_rows * sigmoid
+        hidden[:, low:high] = (silu * up_rows).astype(jnp.bfloat16)
+        back_gate[:tokens, low:high] = (
+            back_hidden * up_rows * sigmoid * (1.0 + gate_rows * (1.0 - sigmoid))
+        ).astype(jnp.bfloat16)
+        back_up[:tokens, low:high] = (back_hidden * silu).astype(jnp.bfloat16)
+        for j, ref in enumerate((back_gate, back_up)):
+            swaps.append(swap(1 + 2 * k + j, ref, pl.ds(low, high - low)))
+            swaps[-1].start()
+
+    def mid_pair(c):
+        cut = pl.ds(c * each, 2 * each)
+        made = nt_dot(back_gate[:tokens, :], gate[cut, :]) + nt_dot(back_up[:tokens, :], up[cut, :])
+        made = made.astype(jnp.bfloat16)
+        term[c] = made[:, :each]
+        term[c + 1] = made[:, each:]
+
+    def mlp_pair(c):
+        made = jnp.dot(
+            hidden[...], down[:, c * each : (c + 2) * each], preferred_element_type=jnp.float32
+        ).astype(jnp.bfloat16)
+        pair = c // 2
+        rows, low = pl.ds(pair % 4 * tokens, tokens), pair // 4 * 2 * each
+        gate[rows, low : low + 2 * each] = made
+        for k in range(2):
+            copy = pltpu.make_async_copy(
+                gate.at[rows, pl.ds(low + k * each, each)], mlp_term.at[c + k], load_sems.at[3, c + k]
+            )
+            copy.start()
+            stores.append(copy)
+
+    stores = []
+    gate_sum = Reduce(own_gate, near_gate, reduce_sems.at[0])
+    up_sum = Reduce(own_up, near_up, reduce_sems.at[1])
+
+    def block(part, k):
+        index = jnp.bitwise_xor(me, 2 * k)
+        cut = pl.ds(pl.multiple_of(index * span, span), span)
+        ref = back_gate if part is gate_sum else back_up
+        part.put(k, tn_dot(normed[:, cut], ref[...]))
+
+    def received(indices):
+        for k in indices:
+            swaps[k].wait_recv()
+
+    pairs_of = lambda n: lambda: (mid_pair(2 * n), mid_pair(count + 2 * n))
+    grad = lambda part, *ks: lambda: [block(part, k) for k in ks]
+    mlp = lambda *cs: lambda: [mlp_pair(2 * c) for c in cs]
+    gates, ups = range(1, len(swaps), 2), range(2, len(swaps), 2)
+    work = {now: [] for now in range(count + 2 * (chain - 1))}
+
+    def plan(now, *jobs):
+        work[min(now, len(work) - 1)].extend(jobs)
+
+    for n in range(count // 2):
+        plan(2 * n, pairs_of(n))
+    plan(1, lambda: received([0, *gates]), grad(gate_sum, 3))
+    plan(3, grad(gate_sum, 1, 2))
+    plan(5, grad(gate_sum, 0), lambda: received(ups), grad(up_sum, 3))
+    plan(7, grad(up_sum, 1), gate_sum.second)
+    plan(8, grad(up_sum, 2))
+    plan(9, grad(up_sum, 0))
+    plan(10, mlp(0, 1, 2, 3))
+    plan(11, up_sum.second)
+    plan(12, mlp(4, 5, 6, 7))
+
+    sums = [
+        ChainSum(chain, upward, term, passing, total, base, count, chain_sems.at[k])
+        for k, (upward, base) in enumerate(((True, 0), (False, count)))
     ]
-    for i in range(count + 2):
-        if i < count:
-            parts[i].start()
-        if 0 <= i - 1 < count:
-            parts[i - 1].cores()
-        if 0 <= i - 2 < count:
-            parts[i - 2].second()
-    for part, out in zip(parts, outs):
-        part.finish(out)
-
-
-def scatter_sums(arrays, axes, collective_id):
-    count = len(arrays)
-    blocks = [
-        tuple(size // 8 if d == axis else size for d, size in enumerate(array.shape))
-        for array, axis in zip(arrays, axes)
-    ]
+    for now, jobs in work.items():
+        for job in jobs:
+            job()
+        for part in sums:
+            part.step(now)
+    gate_sum.finish(grad_gate)
+
+    weighed = jnp.zeros((tokens, each), jnp.float32)
+    for c in range(2 * count):
+        cut = slice(c * each, (c + 1) * each)
+        back = total[c].astype(jnp.float32)
+        hat = middle_at(c) * mid_scale
+        weighed = weighed + back * mid_row[0:1, cut] * hat
+        grad_mid[:, cut] = jnp.broadcast_to(jnp.sum(back * hat, axis=0, keepdims=True), (8, each))
+    mean = jnp.sum(weighed, axis=1, keepdims=True) / width
+    for c in range(2 * count):
+        cut = slice(c * each, (c + 1) * each)
+        u = total[c].astype(jnp.float32) * mid_row[0:1, cut]
+        hat = middle_at(c) * mid_scale
+        back_attn[:, cut] = (
+            cotangent[:, cut].astype(jnp.float32) + mid_scale * (u - hat * mean)
+        ).astype(jnp.bfloat16)
+    up_sum.finish(grad_up)
+    for part in sums:
+        part.finish()
+    for copy in swaps:
+        copy.wait_send()
+    for copy in stores:
+        copy.wait()
+
+
+def feed(chain, x, attn_sum, small_all, cotangent, gate_full, up_full, down_full):
+    tokens, width = x.shape
+    inner = gate_full.shape[1]
+    count = attn_sum.shape[0] // 2
+    span = width // 8
+    bf16, f32 = jnp.bfloat16, jnp.float32
+    anywhere, vmem = pl.BlockSpec(memory_space=pl.ANY), pl.BlockSpec(memory_space=pltpu.VMEM)
+    shape = jax.ShapeDtypeStruct
+    tiles = len(tiles_of(inner, 512))
     return pl.pallas_call(
-        functools.partial(scatter_kernel, axes),
-        out_shape=[jax.ShapeDtypeStruct(s, jnp.float32) for s in blocks],
-        in_specs=[pl.BlockSpec(memory_space=pl.ANY)] * count,
-        out_specs=[pl.BlockSpec(memory_space=pltpu.VMEM)] * count,
-        scratch_shapes=[pltpu.VMEM((4,) + s, a.dtype) for s, a in zip(blocks, arrays)]
-        + [pltpu.VMEM((4,) + s, a.dtype) for s, a in zip(blocks, arrays)]
-        + [pltpu.VMEM((6, s[0] // 2, s[1]), a.dtype) for s, a in zip(blocks, arrays)]
-        + [
-            pltpu.SemaphoreType.DMA((count, 2, Scatter.COPIES)),
-            pltpu.SemaphoreType.DMA((count, 4)),
+        functools.partial(feed_kernel, chain),
+        out_shape=[
+            shape((tokens, width), bf16),
+            shape((tokens, inner), bf16),
+            shape(attn_sum.shape, bf16),
+            shape((span, inner), f32),
+            shape((span, inner), f32),
+            shape((8, width), f32),
+        ],
+        in_specs=[vmem] * 4 + [anywhere] * 3,
+        out_specs=[vmem, vmem, anywhere, vmem, vmem, vmem],
+        scratch_shapes=[
+            pltpu.VMEM((width, inner), bf16),
+            pltpu.VMEM((width, inner), bf16),
+            pltpu.VMEM((inner, width), bf16),
+            pltpu.VMEM((8, width), f32),
+            pltpu.VMEM((2 * tokens, width), bf16),
+            pltpu.VMEM((2 * tokens, inner), bf16),
+            pltpu.VMEM((2 * tokens, inner), bf16),
+            pltpu.VMEM(attn_sum.shape, bf16),
+            pltpu.VMEM(attn_sum.shape, bf16),
+            pltpu.VMEM(attn_sum.shape, bf16),
+            pltpu.VMEM((4, span, inner), bf16),
+            pltpu.VMEM((6, span // 2, inner), bf16),
+            pltpu.VMEM((4, span, inner), bf16),
+            pltpu.VMEM((6, span // 2, inner), bf16),
+            pltpu.SemaphoreType.DMA((4, max(tiles, 2 * count))),
+            pltpu.SemaphoreType.DMA((2, 1 + 2 * tiles)),
+            pltpu.SemaphoreType.DMA((2, 4, count)),
+            pltpu.SemaphoreType.DMA((2, 2, Reduce.COPIES)),
         ],
         compiler_params=pltpu.CompilerParams(
-            collective_id=collective_id, has_side_effects=True, vmem_limit_bytes=VMEM_BYTES
+            collective_id=1, has_side_effects=True, vmem_limit_bytes=VMEM_BYTES
         ),
-        name="scatter_sums",
-    )(*arrays)
+        name="feed_forward",
+    )(x, attn_sum, small_all, cotangent, gate_full, up_full, down_full)
+
+
+def split_marks(values, at):
+    high = values.astype(jnp.bfloat16).astype(jnp.float32)
+    rest = values - high
+    middle = rest.astype(jnp.bfloat16).astype(jnp.float32)
+    low = rest - middle
+    return jnp.where(at == 4, high, jnp.where(at == 5, middle, jnp.where(at == 6, low, 0.0)))
+
+
+def return_kernel(
+    chain, places, small_all, query, pairs, log_total, cos_table, sin_table,
+    mid_part, attended_in, x_in, attn_sum, back_in, in_full, out_full, mlp_term, hidden_in, cotangent, normed_in, layer_out, grad_input, grad_down,
+    grad_in, grad_out, gains, in_here, out_here, key_side, value_side, query_side, back_side, back_att,
+    back_rows, back_keys, back_values, pair_out, pair_near, normed, back_attn, hidden, cotangents, att_low,
+    back_all, pre_row, pre_part, gains_near, mlp_sum, mlp_passing, mlp_total, term, passing, total, own_down,
+    near_down, own_in, near_in, own_out, near_out, load_sems, swap_sems, pair_sems, gain_sems, chain_sems,
+    reduce_sems, store_sems,
+):
+    count = term.shape[0] // 2
+    each = term.shape[2]
+    tokens, width = x_in.shape
+    span = width // 8
+    groups = query.shape[1] // 128
+    me = lax.axis_index("tokens")
+    place = lax.rem(me, places)
+    first_device = me - place
+    mine, theirs = pl.ds(0, tokens), pl.ds(tokens, tokens)
+
+    def load(k, src, dst):
+        copy = pltpu.make_async_copy(src, dst, load_sems.at[k])
+        copy.start()
+        return copy
+
+    attended = back_rows
+    load_attended = load(8 + 2 * count, attended_in, attended)
+    load_back = load(6, back_in, back_attn.at[mine, :])
+    load_out = load(0, out_full, out_here)
+    load_in = load(1, in_full, in_here)
+    load_cot = load(2, cotangent, cotangents.at[mine, :])
+    load_hidden = load(3, hidden_in, hidden.at[mine, :])
+    load_normed = load(4, normed_in, normed.at[mine, :])
+    load_mlp = load(5, mlp_term, mlp_sum)
+    greet(range(1, 8), chain)
+
+    def swap(k, ref):
+        copy = remote(
+            ref.at[mine, :],
+            ref.at[theirs, :],
+            swap_sems.at[0, k],
+            swap_sems.at[1, k],
+            token_device(1),
+        )
+        copy.start()
+        return copy
+
+    def gain_copy(which, src, flip):
+        other = jnp.bitwise_xor(me, flip)
+        return remote(
+            src.at[:, pl.ds(pl.multiple_of(other * span, span), span)],
+            gains_near.at[me, :, pl.ds(which * span, span)],
+            gain_sems.at[0, which, flip - 1],
+            gain_sems.at[1, which, flip - 1],
+            token_device(flip),
+        )
+
+    for flip in range(1, 8):
+        gain_copy(1, mid_part, flip).start()
+    load_back.wait()
+    load_attended.wait()
+    att_low[mine, :] = attended[...].astype(jnp.bfloat16)
+    swap_back = swap(0, back_attn)
+    swap_att = swap(1, att_low)
+
+    lane = lanes((tokens, 128))
+    at = lane % 64
+    first_id = (first_device // places * 4).astype(jnp.float32)
+    for k in range(places):
+        mark = key_marks(token_column(small_all[first_device + k, 0:1, :]), first_id)
+        block = pl.ds(k * tokens, tokens)
+        pair = pairs[block].astype(jnp.float32)
+        swapped = pltpu.roll(pair, 64, 1)
+        key_side[0, block] = jnp.where(lane < 64, pair, mark).astype(jnp.bfloat16)
+        key_side[1, block] = jnp.where(lane < 64, mark, swapped).astype(jnp.bfloat16)
+        value_side[0, block] = jnp.where(lane < 64, swapped, 1.0).astype(jnp.bfloat16)
+        value_side[1, block] = jnp.where(lane < 64, 1.0, pair).astype(jnp.bfloat16)
+    own_marks = query_marks(token_column(small_all[me, 0:1, :]), first_id)
+
+    load_out.wait()
+    back_att[...] = nt_dot(back_attn[mine, :], out_here[...]).astype(jnp.bfloat16)
+    load_cot.wait()
+    swap_cot = swap(2, cotangents)
+    load_hidden.wait()
+    swap_hidden = swap(3, hidden)
+    for group in range(groups):
+        cut = slice(group * 128, (group + 1) * 128)
+        back = back_att[:, cut].astype(jnp.float32)
+        both = query[:, cut].astype(jnp.float32)
+        shared = back * attended[:, cut]
+        for e in range(2):
+            head = 2 * group + e
+            used = (lane < 64) if e == 0 else (lane >= 64)
+            delta = jnp.sum(jnp.where(used, shared, 0.0), axis=1, keepdims=True)
+            peak = jnp.sum(jnp.where(lane == head, log_total[...], 0.0), axis=1, keepdims=True)
+            back_side[head] = jnp.where(
+                used, back, split_marks(jnp.broadcast_to(-delta, lane.shape), at)
+            ).astype(jnp.bfloat16)
+            query_side[head] = jnp.where(
+                used, both, own_marks + split_marks(jnp.broadcast_to(-peak, lane.shape), at)
+            ).astype(jnp.bfloat16)
+    load_normed.wait()
+    swap_normed = swap(4, normed)
+    load_mlp.wait()
+    load_in.wait()
+
+    mlp_sums = [
+        ChainSum(chain, upward, mlp_sum, mlp_passing, mlp_total, base, count, chain_sems.at[0, k])
+        for k, (upward, base) in enumerate(((True, 0), (False, count)))
+    ]
+    back_rows[...] = jnp.zeros_like(back_rows)
+
+    def key_step(k, diagonal):
+        back_keys[...] = jnp.zeros_like(back_keys)
+        back_values[...] = jnp.zeros_like(back_values)
+
+        @pl.loop(0, groups)
+        def _(group):
+            cut = pl.ds(pl.multiple_of(group * 128, 128), 128)
+            for low in (0, tokens // 2):
+                keys_here = pl.ds(pl.multiple_of(k * tokens + low, tokens // 2), tokens // 2)
+                part = pl.ds(low, tokens // 2)
+                first = low if diagonal else 0
+                seen = pl.ds(first, tokens - first)
+                rows = []
+                for e in range(2):
+                    head = 2 * group + e
+                    found = nt_dot(key_side[e, keys_here], query_side[head, seen])
+                    chances = jnp.exp(found)
+                    if diagonal:
+                        keys = lax.broadcasted_iota(jnp.int32, found.shape, 0) + (low - first)
+                        chances = jnp.where(keys <= lanes(found.shape), chances, 0.0)
+                    moved = chances * nt_dot(value_side[e, keys_here], back_side[head, seen])
+                    chances = chances.astype(jnp.bfloat16)
+                    moved = moved.astype(jnp.bfloat16)
+                    back_values[e, part] += jnp.dot(
+                        chances, back_att[seen, cut], preferred_element_type=jnp.float32
+                    )
+                    back_keys[e, part] += jnp.dot(
+                        moved, query[seen, cut], preferred_element_type=jnp.float32
+                    )
+                    rows.append(tn_dot(moved, key_side[e, keys_here]))
+                back_rows[seen, cut] += jnp.where(lanes(rows[0].shape) < 64, rows[0], rows[1])
+
+            @pl.when(group % 2 == 1)
+            def _():
+                for part in mlp_sums:
+                    part.step(2 * k + group // 2)
+
+        keys = back_keys[0] + pltpu.roll(back_keys[1], 64, 1)
+        values = pltpu.roll(back_values[0], 64, 1) + back_values[1]
+        return jnp.where(lane < 64, keys, values)
+
+    def pair_copy(source, target):
+        return remote(
+            pair_out.at[target],
+            pair_near.at[source],
+            pair_sems.at[0, target],
+            pair_sems.at[1, source],
+            (first_device + target, lax.axis_index("heads")),
+        )
+
+    @pl.loop(0, place)
+    def _(k):
+        pair_out[k] = key_step(k, False).astype(jnp.bfloat16)
+        pair_copy(place, k).start()
+
+    own_pair = key_step(place, True)
+    pair_out[place] = own_pair.astype(jnp.bfloat16)
+    early = 2 * places
+
+    @pl.loop(2 * (place + 1), early)
+    def _(now):
+        for part in mlp_sums:
+            part.step(now)
+
+    for group in range(groups):
+        cut = slice(group * 128, (group + 1) * 128)
+        back_all[mine, cut] = (
+            turn(back_rows[:, cut], cos_table[...], -sin_table[...]) * 0.125
+        ).astype(jnp.bfloat16)
+    back_keys[0] = own_pair
+    for k in range(1, places):
+
+        @pl.when(k > place)
+        def _():
+            remote(
+                pair_out.at[k],
+                pair_near.at[k],
+                pair_sems.at[0, k],
+                pair_sems.at[1, k],
+                (first_device + k, lax.axis_index("heads")),
+            ).wait_recv()
+            back_keys[0] += pair_near[k].astype(jnp.float32)
+
+    summed = back_keys[0]
+    spun = turn(summed, cos_table[...], -sin_table[...])
+    back_all[mine, pl.ds(groups * 128, 128)] = jnp.where(lane < 64, spun, summed).astype(
+        jnp.bfloat16
+    )
+    swap_all = swap(5, back_all)
+
+    def pre_pair(c):
+        cut = pl.ds(c * each, 2 * each)
+        made = nt_dot(back_all[mine, :], in_here[cut, :]).astype(jnp.bfloat16)
+        term[c] = made[:, :each]
+        term[c + 1] = made[:, each:]
+
+    def cut_of(k):
+        index = jnp.bitwise_xor(me, 2 * k)
+        return pl.ds(pl.multiple_of(index * span, span), span)
+
+    down_sum = Reduce(own_down, near_down, reduce_sems.at[0])
+    in_sum = Reduce(own_in, near_in, reduce_sems.at[1])
+    out_sum = Reduce(own_out, near_out, reduce_sems.at[2])
+
+    def down_block(k):
+        for low, high in tiles_of(hidden.shape[1], 512):
+            own_down[k, low:high] = tn_dot(hidden[:, low:high], cotangents[:, cut_of(k)]).astype(
+                own_down.dtype
+            )
+        down_sum.send(k)
+
+    def in_block(k):
+        in_sum.put(k, tn_dot(normed[:, cut_of(k)], back_all[...]))
+
+    def out_block(k):
+        out_sum.put(k, tn_dot(att_low[...], back_attn[:, cut_of(k)]))
+
+    def late_loads():
+        copies = [pltpu.make_async_copy(x_in, cotangents.at[theirs, :], load_sems.at[7])]
+        for c in range(2 * count):
+            copies.append(
+                pltpu.make_async_copy(
+                    attn_sum.at[c],
+                    cotangents.at[mine, pl.ds(c * each, each)],
+                    load_sems.at[8 + c],
+                )
+            )
+        return copies
+
+    def load_late():
+        swap_cot.wait_send()
+        for copy in late_loads():
+            copy.start()
+
+    def x_at(c):
+        return cotangents[theirs, c * each : (c + 1) * each].astype(jnp.float32)
+
+    def middle_at(c):
+        return x_at(c) + cotangents[mine, c * each : (c + 1) * each].astype(jnp.float32)
+
+    stores = []
+
+    def store(c, src, out):
+        copy = pltpu.make_async_copy(
+            src.at[c], out.at[:, pl.ds(c * each, each)], store_sems.at[len(stores)]
+        )
+        copy.start()
+        stores.append(copy)
+
+    def finish_mlp():
+        for part in mlp_sums:
+            part.finish()
+        for copy in late_loads():
+            copy.wait()
+        for c in range(2 * count):
+            mlp_sum[c] = (middle_at(c) + mlp_total[c].astype(jnp.float32)).astype(jnp.bfloat16)
+            store(c, mlp_sum, layer_out)
+
+    def scale_rows():
+        for k in range(8):
+            pre_row[:, k * span : (k + 1) * span] = jnp.broadcast_to(
+                small_all[k, 1:2, :span], (8, span)
+            )
+
+    steps = count + 2 * (chain - 1)
+    work = {now: [] for now in range(steps)}
+
+    def plan(now, *jobs):
+        work[min(now, steps - 1)].extend(jobs)
+
+    pre = lambda n: lambda: (pre_pair(2 * n), pre_pair(count + 2 * n))
+    blocks = lambda make, *ks: lambda: [make(k) for k in ks]
+    received = lambda *copies: lambda: [copy.wait_recv() for copy in copies]
+    for n in range(count // 2):
+        plan(2 * n, pre(n))
+    plan(1, received(swap_cot, swap_hidden), blocks(down_block, 3, 1))
+    plan(3, blocks(down_block, 2, 0), load_late)
+    plan(4, received(swap_back, swap_att), blocks(out_block, 3, 1, 2, 0))
+    plan(5, received(swap_normed, swap_all), blocks(in_block, 3, 1, 2, 0))
+    plan(7, down_sum.second)
+    plan(8, finish_mlp)
+    plan(9, out_sum.second)
+    plan(10, in_sum.second, scale_rows)
+    plan(11, lambda: down_sum.finish(grad_down))
+    plan(12, lambda: out_sum.finish(grad_out))
+    sums = [
+        ChainSum(chain, upward, term, passing, total, base, count, chain_sems.at[1, k])
+        for k, (upward, base) in enumerate(((True, 0), (False, count)))
+    ]
+    for now, jobs in work.items():
+        for job in jobs:
+            job()
+        if early + now < steps:
+            for part in mlp_sums:
+                part.step(early + now)
+        for part in sums:
+            part.step(now)
+    for part in sums:
+        part.finish()
+
+    squares = jnp.zeros((tokens, each), jnp.float32)
+    for c in range(2 * count):
+        part = x_at(c)
+        squares = squares + part * part
+    pre_scale = lax.rsqrt(jnp.sum(squares, axis=1, keepdims=True) / width + 1e-05)
+    weighed = jnp.zeros((tokens, each), jnp.float32)
+    for c in range(2 * count):
+        cut = slice(c * each, (c + 1) * each)
+        back = total[c].astype(jnp.float32)
+        hat = x_at(c) * pre_scale
+        weighed = weighed + back * pre_row[0:1, cut] * hat
+        pre_part[:, cut] = jnp.broadcast_to(jnp.sum(back * hat, axis=0, keepdims=True), (8, each))
+    for flip in range(1, 8):
+        gain_copy(0, pre_part, flip).start()
+    mean = jnp.sum(weighed, axis=1, keepdims=True) / width
+    for c in range(2 * count):
+        cut = slice(c * each, (c + 1) * each)
+        u = total[c].astype(jnp.float32) * pre_row[0:1, cut]
+        hat = x_at(c) * pre_scale
+        term[c] = (
+            back_attn[mine, cut].astype(jnp.float32) + pre_scale * (u - hat * mean)
+        ).astype(jnp.bfloat16)
+        store(c, term, grad_input)
+    in_sum.finish(grad_in)
+    own = pl.ds(pl.multiple_of(me * span, span), span)
+    gains_near[me, :, :span] = pre_part[:, own]
+    gains_near[me, :, span:] = mid_part[:, own]
+    for flip in range(1, 8):
+        for which, src in enumerate((pre_part, mid_part)):
+            gain_copy(which, src, flip).wait_recv()
+    gains[...] = jnp.sum(gains_near[...], axis=0)
+    for flip in range(1, 8):
+        for which, src in enumerate((pre_part, mid_part)):
+            gain_copy(which, src, flip).wait_send()
+    for copy in (swap_back, swap_att, swap_hidden, swap_normed, swap_all):
+        copy.wait_send()
+
+    @pl.loop(0, place)
+    def _(k):
+        pair_copy(place, k).wait_send()
+
+    for copy in stores:
+        copy.wait()
+
+
+def way_back(
+    chain, places, x, attn_sum, small_all, back_attn, query, pairs, attended, log_total, cos_table, sin_table,
+    mid_part, in_full, out_full, mlp_term, hidden, cotangent, normed,
+):
+    tokens, width = x.shape
+    inner = hidden.shape[1]
+    heads_wide = query.shape[1]
+    wide = in_full.shape[1]
+    chunks = attn_sum.shape
+    count = chunks[0] // 2
+    span = width // 8
+    row = places * tokens
+    bf16, f32 = jnp.bfloat16, jnp.float32
+    anywhere, vmem = pl.BlockSpec(memory_space=pl.ANY), pl.BlockSpec(memory_space=pltpu.VMEM)
+    shape = jax.ShapeDtypeStruct
+    return pl.pallas_call(
+        functools.partial(return_kernel, chain, places),
+        out_shape=[
+            shape((tokens, width), bf16),
+            shape((tokens, width), bf16),
+            shape((inner, span), f32),
+            shape((span, wide), f32),
+            shape((heads_wide, span), f32),
+            shape((8, 2 * span), f32),
+        ],
+        in_specs=[vmem] * 7 + [anywhere] * 10,
+        out_specs=[anywhere] * 2 + [vmem] * 4,
+        scratch_shapes=[
+            pltpu.VMEM((width, wide), bf16),
+            pltpu.VMEM((heads_wide, width), bf16),
+            pltpu.VMEM((2, row, 128), bf16),
+            pltpu.VMEM((2, row, 128), bf16),
+            pltpu.VMEM((heads_wide // 64, tokens, 128), bf16),
+            pltpu.VMEM((heads_wide // 64, tokens, 128), bf16),
+            pltpu.VMEM((tokens, heads_wide), bf16),
+            pltpu.VMEM((tokens, heads_wide), f32),
+            pltpu.VMEM((2, tokens, 128), f32),
+            pltpu.VMEM((2, tokens, 128), f32),
+            pltpu.VMEM((places, tokens, 128), bf16),
+            pltpu.VMEM((places, tokens, 128), bf16),
+            pltpu.VMEM((2 * tokens, width), bf16),
+            pltpu.VMEM((2 * tokens, width), bf16),
+            pltpu.VMEM((2 * tokens, inner), bf16),
+            pltpu.VMEM((2 * tokens, width), bf16),
+            pltpu.VMEM((2 * tokens, heads_wide), bf16),
+            pltpu.VMEM((2 * tokens, wide), bf16),
+            pltpu.VMEM((8, width), f32),
+            pltpu.VMEM((8, width), f32),
+            pltpu.VMEM((8, 8, 2 * span), f32),
+            pltpu.VMEM(chunks, bf16),
+            pltpu.VMEM(chunks, bf16),
+            pltpu.VMEM(chunks, bf16),
+            pltpu.VMEM(chunks, bf16),
+            pltpu.VMEM(chunks, bf16),
+            pltpu.VMEM(chunks, bf16),
+            pltpu.VMEM((4, inner, span), bf16),
+            pltpu.VMEM((6, inner // 2, span), bf16),
+            pltpu.VMEM((4, span, wide), bf16),
+            pltpu.VMEM((6, span // 2, wide), bf16),
+            pltpu.VMEM((4, heads_wide, span), bf16),
+            pltpu.VMEM((6, heads_wide // 2, span), bf16),
+            pltpu.SemaphoreType.DMA((9 + 2 * count,)),
+            pltpu.SemaphoreType.DMA((2, 6)),
+            pltpu.SemaphoreType.DMA((2, places)),
+            pltpu.SemaphoreType.DMA((2, 2, 7)),
+            pltpu.SemaphoreType.DMA((2, 2, 4, count)),
+            pltpu.SemaphoreType.DMA((3, 2, Reduce.COPIES)),
+            pltpu.SemaphoreType.DMA((4 * count,)),
+        ],
+        compiler_params=pltpu.CompilerParams(
+            collective_id=2, has_side_effects=True, vmem_limit_bytes=VMEM_BYTES
+        ),
+        name="way_back",
+    )(
+        small_all, query, pairs, log_total, cos_table, sin_table,
+        mid_part, attended, x, attn_sum, back_attn, in_full, out_full, mlp_term, hidden, cotangent, normed,
+    )
 
 
 def shards_cube(
@@ -1054,159 +1598,34 @@
     ) = attend(
         chain, places, inputs, small, in_weight, out_weight, gate_weight, up_weight, down_weight, inverse
     )
-    query_full = in_full[:, :query_width]
-    key_full = in_full[:, query_width : query_width + head_size]
-    value_full = in_full[:, query_width + head_size :]
-    all_ids = small_full[:, 0].reshape(-1).astype(jnp.int32)
-    pre_row = small_full[:, 1, : row_count // 2].reshape(-1)
-    mid_row = small_full[:, 1, row_count // 2 :].reshape(-1)
-    myself = lax.axis_index("tokens")
-    own_first = myself * row_count
-    own_places = own_first + jnp.arange(row_count, dtype=jnp.int32)
-    row_start = own_first // ROW * ROW
-    length = all_ids.shape[0]
-    span = math.gcd(ROW, 1024)
-    block_first = row_start // span
-    block_total = (own_first + row_count + span - 1) // span
-    key_all = lax.dynamic_update_slice_in_dim(
-        jnp.zeros((length, head_size), jnp.bfloat16), pairs[:, :head_size], row_start, 0
-    )
-    value_all = lax.dynamic_update_slice_in_dim(
-        jnp.zeros((length, head_size), jnp.bfloat16), pairs[:, head_size:], row_start, 0
-    )
-    cos_table = cos_wide[:, None, :half_size]
-    sin_table = sin_wide[:, None, half_size : 2 * half_size]
-    inputs_f = inputs.astype(jnp.float32)
-    pre_scale = rms_scale(inputs_f)
-    attended_low = attended.astype(jnp.bfloat16)
-    attended = attended.reshape(row_count, heads_here, head_size)
-    query_rot = query_rot.reshape(row_count, heads_here, head_size)
-    log_total = log_total[:, :heads_here]
-
-    def key_block(block_index):
-        opening_row = block_index * span
-        block_keys = lax.dynamic_slice_in_dim(key_all, opening_row, span)
-        block_values = lax.dynamic_slice_in_dim(value_all, opening_row, span)
-        block_ids = lax.dynamic_slice_in_dim(all_ids, opening_row, span)
-        block_places = opening_row + jnp.arange(span, dtype=jnp.int32)
-        allowed = (segments[:, None] == block_ids[None, :]) & (
-            own_places[:, None] >= block_places[None, :]
-        )
-        scores = jnp.einsum(
-            "qhd,kd->qhk", query_rot, block_keys, preferred_element_type=jnp.float32
-        )
-        return (opening_row, block_keys, block_values, allowed[:, None, :], scores)
-
-    attn_term = attn_sum.transpose(1, 0, 2).reshape(row_count, -1)
-    middle = inputs_f + attn_term.astype(jnp.float32)
-    mid_scale = rms_scale(middle)
-    normed_mid = (middle * mid_scale * mid_row).astype(jnp.bfloat16)
-    gate_rows = jnp.dot(normed_mid, gate_full, preferred_element_type=jnp.float32)
-    up_rows = jnp.dot(normed_mid, up_full, preferred_element_type=jnp.float32)
-    sigmoid_rows = jax.nn.sigmoid(gate_rows)
-    silu_rows = gate_rows * sigmoid_rows
-    hidden = (silu_rows * up_rows).astype(jnp.bfloat16)
-    mlp_term = jnp.dot(hidden, down_full, preferred_element_type=jnp.float32)
-    layer_out = (
-        middle + chain_sum(mlp_term.astype(jnp.bfloat16), chain, 2).astype(jnp.float32)
-    ).astype(jnp.bfloat16)
-    grad_down = jnp.einsum("tf,td->fd", hidden, cotangent, preferred_element_type=jnp.float32)
-    back_hidden = jnp.einsum("td,fd->tf", cotangent, down_full, preferred_element_type=jnp.float32)
-    back_gate = (
-        back_hidden * up_rows * sigmoid_rows * (1.0 + gate_rows * (1.0 - sigmoid_rows))
-    ).astype(jnp.bfloat16)
-    back_up = (back_hidden * silu_rows).astype(jnp.bfloat16)
-    grad_gate = jnp.einsum("tc,tf->cf", normed_mid, back_gate, preferred_element_type=jnp.float32)
-    grad_up = jnp.einsum("tc,tf->cf", normed_mid, back_up, preferred_element_type=jnp.float32)
-    mid_term = jnp.einsum(
-        "tf,cf->tc", back_gate, gate_full, preferred_element_type=jnp.float32
-    ) + jnp.einsum("tf,cf->tc", back_up, up_full, preferred_element_type=jnp.float32)
-    back_normed_mid = chain_sum(mid_term.astype(jnp.bfloat16), chain, 3).astype(jnp.float32)
-    back_middle, grad_mid = norm_back(back_normed_mid, middle, mid_scale, mid_row)
-    back_middle = back_middle + cotangent.astype(jnp.float32)
-    back_attn = back_middle.astype(jnp.bfloat16)
-    grad_out = jnp.einsum("tc,td->cd", attended_low, back_attn, preferred_element_type=jnp.float32)
-    back_attended = (
-        jnp.einsum("td,cd->tc", back_attn, out_full, preferred_element_type=jnp.float32)
-        .astype(jnp.bfloat16)
-        .reshape(row_count, heads_here, head_size)
-    )
-    row_delta = jnp.sum(back_attended.astype(jnp.float32) * attended, axis=-1)
-
-    def backward_step(block_index, state_now):
-        back_rows, back_pairs = state_now
-        opening_row, block_keys, block_values, allowed, scores = key_block(block_index)
-        chances = jnp.where(allowed, jnp.exp(scores - log_total[..., None]), 0.0)
-        back_values = jnp.einsum(
-            "qhk,qhd->kd",
-            chances.astype(jnp.bfloat16),
-            back_attended,
-            preferred_element_type=jnp.float32,
-        )
-        back_chances = jnp.einsum(
-            "qhd,kd->qhk", back_attended, block_values, preferred_element_type=jnp.float32
-        )
-        back_scores = (chances * (back_chances - row_delta[..., None])).astype(jnp.bfloat16)
-        back_rows = back_rows + jnp.einsum(
-            "qhk,kd->qhd", back_scores, block_keys, preferred_element_type=jnp.float32
-        )
-        back_keys = jnp.einsum(
-            "qhk,qhd->kd", back_scores, query_rot, preferred_element_type=jnp.float32
-        )
-        old_piece = lax.dynamic_slice_in_dim(back_pairs, opening_row, span)
-        fresh_piece = old_piece + jnp.concatenate([back_keys, back_values], axis=-1)
-        back_pairs = lax.dynamic_update_slice_in_dim(back_pairs, fresh_piece, opening_row, 0)
-        return (back_rows, back_pairs)
-
-    start_back = (
-        jnp.zeros((row_count, heads_here, head_size), jnp.float32),
-        jnp.zeros((length, 2 * head_size), jnp.float32),
-    )
-    back_rows, back_pairs = lax.fori_loop(block_first, block_total, backward_step, start_back)
-    own_pairs = lax.psum_scatter(
-        back_pairs.astype(jnp.bfloat16), "tokens", scatter_dimension=0, tiled=True
-    ).astype(jnp.float32)
-    back_query = (
-        (unrotate(back_rows, cos_table, sin_table) * head_size ** (-0.5))
-        .astype(jnp.bfloat16)
-        .reshape(row_count, heads_here * head_size)
-    )
-    back_key = unrotate(own_pairs[:, None, :head_size], cos_table, sin_table)[:, 0, :].astype(
-        jnp.bfloat16
-    )
-    back_value = own_pairs[:, head_size:].astype(jnp.bfloat16)
-    grad_query = jnp.einsum("tc,tq->cq", normed, back_query, preferred_element_type=jnp.float32)
-    grad_key = jnp.einsum("tc,tq->cq", normed, back_key, preferred_element_type=jnp.float32)
-    grad_value = jnp.einsum("tc,tq->cq", normed, back_value, preferred_element_type=jnp.float32)
-    pre_term = jnp.einsum("tq,cq->tc", back_query, query_full, preferred_element_type=jnp.float32)
-    pre_term = pre_term + jnp.einsum(
-        "tq,cq->tc", back_key, key_full, preferred_element_type=jnp.float32
-    )
-    pre_term = pre_term + jnp.einsum(
-        "tq,cq->tc", back_value, value_full, preferred_element_type=jnp.float32
-    )
-    back_normed = chain_sum(pre_term.astype(jnp.bfloat16), chain, 4).astype(jnp.float32)
-    back_inputs, grad_pre = norm_back(back_normed, inputs_f, pre_scale, pre_row)
-    grad_input = (back_middle + back_inputs).astype(jnp.bfloat16)
-    grad_in = jnp.concatenate([grad_query, grad_key, grad_value], axis=1).astype(jnp.bfloat16)
-    grad_gate, grad_up, grad_down, grad_in, grad_out = scatter_sums(
-        (
-            grad_gate.astype(jnp.bfloat16),
-            grad_up.astype(jnp.bfloat16),
-            grad_down.astype(jnp.bfloat16),
-            grad_in,
-            grad_out.astype(jnp.bfloat16),
-        ),
-        (0, 0, 1, 0, 1),
-        5,
-    )
+    back_attn, hidden, mlp_term, grad_gate, grad_up, grad_mid = feed(
+        chain, inputs, attn_sum, small_full, cotangent, gate_full, up_full, down_full
+    )
+    layer_out, grad_input, grad_down, grad_in, grad_out, gains = way_back(
+        chain,
+        places,
+        inputs,
+        attn_sum,
+        small_full,
+        back_attn,
+        query_rot,
+        pairs,
+        attended,
+        log_total,
+        cos_wide,
+        sin_wide,
+        grad_mid,
+        in_full,
+        out_full,
+        mlp_term,
+        hidden,
+        cotangent,
+        normed,
+    )
+    grad_pre, grad_mid = jnp.split(gains[0], 2)
     grad_query = grad_in[:, :query_width]
     grad_key = grad_in[:, query_width : query_width + head_size]
     grad_value = grad_in[:, query_width + head_size :]
-    grad_pre, grad_mid = (
-        lax.psum_scatter(part.astype(jnp.bfloat16), "tokens", scatter_dimension=0, tiled=True).astype(jnp.float32)
-        for part in (grad_pre, grad_mid)
-    )
     return (
         layer_out,
         grad_input,

time: 717 us -> 391 us (0.55)
  matrix products: 107 us -> 0 us
  Pallas kernels: 429 us -> 360 us
  other arithmetic: 54.1 us -> 3.15 us
  local copies, waits for them, and re-layouts: 58.5 us -> 19.2 us
  waiting for transfers between devices: 30.3 us -> 0 us
  between operations: 15.5 us -> 0.93 us
  blocking collectives: 12.1 us -> 0 us
    dot_general x22 -> x0, matrix products: 107 us -> none  [the longest x1 9.55 us: shards_cube(): up_rows = jnp.dot(normed_mid, up_full, preferred_element_type=jnp.float32)]
    pallas_call x4 -> x2, Pallas kernels: 299 us -> 230 us  [the longest x1 134 us: way_back(): pl.pallas_call(functools.partial(return_kernel, chain, places), out_shape...]
    reduce_scatter x1 -> x0, waiting for transfers between devices: 30.3 us -> none  [shards_cube(): lax.psum_scatter(back_pairs.astype(jnp.bfloat16), 'tokens', scatter_dimen...]
    convert_element_type x11 -> x0, other arithmetic: 27 us -> none  [the longest x1 5.02 us: shards_cube(): grad_input = (back_middle + back_inputs).astype(jnp.bfloat16)]
    convert_element_type x4 -> x0, local copies, waits for them, and re-layouts: 22.3 us -> none  [the longest x1 5.87 us: shards_cube(): middle = inputs_f + attn_term.astype(jnp.float32)]
    unnamed x1 -> x0, blocking collectives: 12.1 us -> none
    reduce_sum x3 -> x0, other arithmetic: 10.9 us -> none  [the longest x2 7.74 us: norm_back(): return (back_vectors, jnp.sum(gradient * shaped, axis=0))]
    unnamed x96 -> x20, local copies, waits for them, and re-layouts: 21 us -> 12.8 us
  transfers between devices with their start and end apart: 1 -> 0, of which waited for: 1 -> 0; matrix products, arithmetic and copies ran while one was open for 5% -> 0% of each run, Pallas kernels for 0% -> 0%
where the time goes in v3:
time: 391 us; the launch traced here: 383 us
  Pallas kernels  360 us (92%)
  local copies, waits for them, and re-layouts  19.2 us (5%)
    pallas_call x1, Pallas kernels, way_back(): pl.pallas_call(functools.partial(return_kernel, chain, places), out_shape...  134 us
    pallas_call x1, Pallas kernels, attend(): pl.pallas_call(functools.partial(attend_kernel, chain, places), out_shape...  130 us
    pallas_call x1, Pallas kernels, feed(): pl.pallas_call(functools.partial(feed_kernel, chain), out_shape=[shape((t...  96 us
    unnamed x20, local copies, waits for them, and re-layouts  12.8 us

profile of v3, /device:TPU:0, one launch (start us, length us, event | category | flops | bytes accessed | tf_op | source)
XLA Modules:
  0.0 383.0 jit_solution(6639126811782227292)
XLA Ops:
  0.7 0.1 pad.5.clone
  0.7 0.7 concatenate.20
  1.4 0.7 concatenate.21
  2.1 0.1 broadcast_in_dim.11
  2.2 0.7 convert_element_type.13
  2.8 0.6 broadcast_in_dim.12.inverse
  3.4 0.7 maximum_maximum_fusion.small
  4.1 0.9 copy.23
  5.0 0.9 copy.24
  5.9 1.8 pad_maximum_fusion.in_shard
  7.6 129.8 %attend_forward.1 = (bf16[2048,1408]{1,0:T(8,128)(2,1)}, bf16[2048,1408]{1,0:T(8,128)(2,1)}, bf16[1408,2048]{1,0:T(8,128)(2,1)}, bf16[2048,640]{1,0:T(8,128)(2,1...) custom-call(bf16[512,2048]{1,0:T(8,128)(2,1)} %x_in.1, ...), custom_call_target="tpu_custom_call" | custom-call | tf_op jit(solution)/shard_map/attend_forward/pallas_call | solution.py:761
  137.4 96.0 %feed_forward.1 = (bf16[512,2048]{1,0:T(8,128)(2,1)}, bf16[512,1408]{1,0:T(8,128)(2,1)}, bf16[16,512,128]{2,1,0:T(8,128)(2,1)}, f32[256,1408]{1,0:T(8,128)}, f32[256,1408]{1,0:T(8,128)}, /*index=5*/f32[8,2048]{1,0:T(8,128)}) custom-call(bf16[512,2048]{1,0:T(8,128)(2,1)} %x_in.1, bf16[16,512,128]{2,1,0:T(8,128)(2,1)} %get-tuple-element.43.attn_sum, ...), custom_call_target="tpu_custom_call" | custom-call | tf_op jit(solution)/shard_map/feed_forward/pallas_call | solution.py:1070
  233.4 134.0 %way_back.1 = (bf16[512,2048]{1,0:T(8,128)(2,1)}, bf16[512,2048]{1,0:T(8,128)(2,1)}, f32[1408,256]{1,0:T(8,128)}, f32[256,640]{1,0:T(8,128)}, f32[512,256]{1,0:T(8,128)}, /*index=5*/f32[8,512]{1,0:T(8,128)}) custom-call(f32[8,8,512]{2,1,0:T(8,128)} %get-tuple-element.37.small_all, bf16[512,512]{1,0:T(8,128)(2,1)} %get-tuple-element.38.query, ...), custom_call_target="tpu_custom_call" | custom-call | tf_op jit(solution)/shard_map/way_back/pallas_call | solution.py:1488
  367.4 1.3 fusion.1
  368.7 1.1 fusion
  369.8 1.9 slice.14
  371.7 0.7 copy.26
  372.4 0.7 copy.25
  373.1 0.0 copy-start
  373.1 3.3 copy.33
  376.4 0.0 copy-done
  376.4 0.0 copy-start.4
  376.4 0.0 copy-start.2
  376.4 1.3 copy.34
  377.7 0.1 copy-done.4
  377.8 0.0 copy-start.1
  377.8 0.8 copy.35
  378.6 0.1 copy-done.2
  378.7 1.1 copy.36
  379.8 0.0 copy-done.1
  379.8 0.0 copy-start.3
  379.8 1.1 copy.37
  380.9 0.8 copy-done.3
  381.7 1.1 copy.38
  (4 shorter events, 0.0 us)
Async XLA Ops:
  373.1 3.3 copy-start
  376.4 1.4 copy-start.4
  376.4 2.3 copy-start.2
  377.8 2.0 copy-start.1
  379.8 1.9 copy-start.3
